TPU v7x, 128 devices: a whole 4x4x4 slice. The times are simulated.
128 devices in a mesh: row: 16 (over z, y_hi, core), col: 8 (over y_lo, x).
Axes of the slice: x: 4, y: 4 (y_hi: 2, y_lo: 2; y = y_hi * 2 + y_lo), z: 4, core: 2. Of those that a mesh axis runs over, the one named last changes fastest.
Arguments:
- tokens: bfloat16 [1024, 6144], P('col', 'row'), may hold values from -160 to 160
- ln_gain: float32 [6144], P('row'), may hold values from 0.5 to 1.5
- w_up: bfloat16 [6144, 24576], P('row', 'col'), may hold values from -0.078125 to 0.078125
- w_down: bfloat16 [24576, 6144], P('col', 'row'), may hold values from -0.0390625 to 0.0390625
- proj: bfloat16 [6144, 256], P('row'), may hold values from -0.078125 to 0.078125
- conv_kernel: bfloat16 [3, 3, 256, 256], replicated, may hold values from -0.125 to 0.125
- head_weight: float32 [256], replicated, may hold values from -0.375 to 0.375
- depth_mm: int32 [16, 64], P('col'), may hold values from 1000 to 80000
- lidar_mask: int32 [16, 64], P('col'), may hold values from 0 to 1, as said below
Outputs:
- grad_up: float32 [6144, 24576], P('row', 'col')
- grad_down: float32 [24576, 6144], P('col', 'row')
- loss: float32 [], replicated
Inputs may be any that keep to these rules, and one draw needn't show every extreme that they name: `lidar_mask`: at least one entry is 1.
All inputs are finite; a program needn't handle non-finite values.
Results may differ from a plain program's by a relative error of at most 0.04.
Values may be sent and summed in bfloat16 or wider, within the bound.
A program may use at most 128 MiB of HBM per device.

v0:
```python
import jax
import jax.numpy as jnp
from jax import lax
from jax.sharding import PartitionSpec as P

D = 6144
GW = 64


variance_focus = 0.85
norm_eps = 1e-06


def extended(cells, sides, width):
    for axis, dim in sides:
        count = lax.axis_size(axis)
        ends = count - 1
        head = lax.slice_in_dim(cells, 0, width, axis=dim)
        tail = lax.slice_in_dim(cells, cells.shape[dim] - width, cells.shape[dim], axis=dim)
        cells = jnp.concatenate(
            [
                lax.ppermute(tail, axis, [(i, (i + 1) % count) for i in range(ends)]),
                cells,
                lax.ppermute(head, axis, [((i + 1) % count, i) for i in range(ends)]),
            ],
            axis=dim,
        )
    return cells


def normalize(values, first, second, gain, width):
    mean = first / width
    spread = second / width - mean * mean
    return (values - mean[:, None]) * lax.rsqrt(spread + norm_eps)[:, None] * gain[None, :]


def gelu_exact(values):
    return jax.nn.gelu(values, approximate=False)


def gelu_back(pre, cotangent):
    _, pull = jax.vjp(gelu_exact, pre)
    return pull(cotangent)[0]


def neighbours(field, offsets):
    height = field.shape[0] - 2
    across = field.shape[1] - 2
    return jnp.concatenate(
        [field[a : a + height, b : b + across, :].reshape(height * across, -1) for a, b in offsets],
        axis=1,
    )


def on_device(tokens, ln_gain, w_up, w_down, proj, conv_kernel, head_weight, depth_mm, lidar_mask):
    strip_tokens = tokens.shape[0]
    xf_own = tokens.astype(jnp.float32)
    rows_all = lax.all_gather(tokens, "col", axis=0, tiled=True)
    xf_all = rows_all.astype(jnp.float32)
    first, second = lax.psum((jnp.sum(xf_all, 1), jnp.sum(xf_all * xf_all, 1)), "row")
    normed = normalize(xf_all, first, second, ln_gain, D).astype(jnp.bfloat16)
    total = normed.shape[0]
    row_count = lax.axis_size("row")

    def back_term_of(grad_rows):

        def back_term(start, count):
            return lax.dot_general(
                grad_rows, w_down, (((1,), (1,)), ((), ())), preferred_element_type=jnp.float32
            )

        return back_term

    pre_share = lax.psum_scatter(
        jnp.dot(normed, w_up, preferred_element_type=jnp.float32).astype(jnp.bfloat16),
        "row",
        scatter_dimension=0,
        tiled=True,
    ).astype(jnp.float32)
    hidden = lax.all_gather(gelu_exact(pre_share).astype(jnp.bfloat16), "row", axis=0, tiled=True)
    out = lax.psum_scatter(
        jnp.dot(hidden, w_down, preferred_element_type=jnp.float32).astype(jnp.bfloat16),
        "col",
        scatter_dimension=0,
        tiled=True,
    ).astype(jnp.float32)
    mixed = (xf_own + out).astype(jnp.bfloat16)
    z = lax.psum(
        jnp.dot(mixed, proj, preferred_element_type=jnp.float32).astype(jnp.bfloat16), "row"
    ).astype(jnp.float32)
    strip_rows = strip_tokens // GW
    channels = z.shape[1]
    forward_offsets = [(i, j) for i in range(3) for j in range(3)]
    backward_offsets = [(2 - i, 2 - j) for i in range(3) for j in range(3)]
    act = gelu_exact(z).astype(jnp.bfloat16).reshape(strip_rows, GW, channels)
    padded = extended(act, (("col", 0),), 1)
    padded = jnp.pad(padded, ((0, 0), (1, 1), (0, 0)))
    u_field = z + jnp.dot(
        neighbours(padded, forward_offsets),
        conv_kernel.reshape(9 * channels, channels),
        preferred_element_type=jnp.float32,
    )
    pred = jnp.dot(u_field, head_weight, precision=lax.Precision.HIGHEST)
    valid = lidar_mask.reshape(-1).astype(jnp.float32)
    target = jnp.log(depth_mm.reshape(-1).astype(jnp.float32) * 0.001)
    err = valid * (pred - target)
    count, sum_err, sum_square = lax.psum((jnp.sum(valid), jnp.sum(err), jnp.sum(err * err)), "col")
    mean_err = sum_err / count
    loss = sum_square / count - variance_focus * mean_err * mean_err
    grad_pred = valid * (2.0 * err - 2.0 * variance_focus * mean_err)
    grad_u = grad_pred[:, None] * head_weight[None, :]
    grad_field = grad_u.astype(jnp.bfloat16).reshape(strip_rows, GW, channels)
    grad_pad = extended(grad_field, (("col", 0),), 1)
    grad_pad = jnp.pad(grad_pad, ((0, 0), (1, 1), (0, 0)))
    back_kernel = jnp.swapaxes(conv_kernel, 2, 3).reshape(9 * channels, channels)
    back_conv = jnp.dot(
        neighbours(grad_pad, backward_offsets), back_kernel, preferred_element_type=jnp.float32
    )
    grad_z = grad_u + gelu_back(z, back_conv)
    grad_mixed = jnp.dot(
        grad_z.astype(jnp.bfloat16), proj.T, preferred_element_type=jnp.float32
    ).astype(jnp.bfloat16)
    grad_rows = lax.all_gather(grad_mixed, "col", axis=0, tiled=True)
    grad_down = lax.dot_general(
        hidden, grad_rows, (((0,), (0,)), ((), ())), preferred_element_type=jnp.float32
    )
    back_term = back_term_of(grad_rows)
    back_share = lax.psum_scatter(
        back_term(jnp.int32(0), lax.axis_size("row") * (total // row_count)).astype(jnp.bfloat16),
        "row",
        scatter_dimension=0,
        tiled=True,
    ).astype(jnp.float32)
    grad_pre = lax.all_gather(
        gelu_back(pre_share, back_share).astype(jnp.bfloat16), "row", axis=0, tiled=True
    )
    grad_up = lax.dot_general(
        normed, grad_pre, (((0,), (0,)), ((), ())), preferred_element_type=jnp.float32
    )
    return (grad_up, grad_down, loss)


def solution(mesh):
    return jax.shard_map(
        on_device,
        mesh=mesh,
        in_specs=(
            P("col", "row"),
            P("row"),
            P("row", "col"),
            P("col", "row"),
            P("row", None),
            P(),
            P(),
            P("col", None),
            P("col", None),
        ),
        out_specs=(P("row", "col"), P("col", "row"), P()),
        check_vma=False,
    )
```

profile of v0, /device:TPU:1, one launch (start us, length us, event | category | flops | bytes accessed | tf_op | source)
XLA Modules:
  0.0 664.8 jit_solution(6059767849232747431)
XLA Ops:
  7.2 25.9 %all_gather.12 = bf16[1024,384]{1,0:T(8,128)(2,1)S(1)} all-gather(bf16[128,384]{1,0:T(8,128)(2,1)} %param.9), channel_id=1, replica_groups=mesh['row'=16,'col'=8] {'col'}, dimensions={0}, use_global_device_ids=true | all-gather | bytes 884736 | tf_op jit(solution)/shard_map/all_gather | solution.py:58
  33.5 40.2 %all-reduce.2 = (f32[1024]{0:T(1024)S(1)}, f32[1024]{0:T(1024)S(1)}) all-reduce(f32[1024]{0:T(1024)S(1)} %get-tuple-element.4, f32[1024]{0:T(1024)S(1)} %get-tuple-element.3), channel_id=1, replica_groups=mesh['row'=16,'col'=8] {'row'}, use_global_device_ids=true, to_apply=%region_3.0 | all-reduce | flops 2048 | bytes 16384 | tf_op jit(solution)/shard_map/psum | solution.py:60
  73.7 7.3 %convolution_convert_fusion.1 = bf16[1024,3072]{1,0:T(8,128)(2,1)} fusion(bf16[384,3072]{1,0:T(8,128)(2,1)} %param.11, bf16[1024,384]{1,0:T(8,128)(2,1)S(1)} %all_gather.12, f32[384]{0:T(512)} %param.10, f32[1024]{0:T(1024)S(1)} %get-tuple-element.37, f32[1024]{0:T(1024)S(1)} %get-tuple-element.36), kind=kOutput, calls=%fused_computation.1 | convolution fusion | flops 2421030912 | bytes 9446912 | tf_op jit(solution)/shard_map/dot_general | solution.py:75
  81.1 84.3 %reduce-scatter.4.cloned.1.call-done = bf16[64,3072]{1,0:T(8,128)(2,1)} async-done(((bf16[1024,3072]{1,0:T(8,128)(2,1)}), bf16[64,3072]{1,0:T(8,128)(2,1)}) %reduce-scatter.4.cloned.1.call-update) | async-done | bytes 393232 | tf_op jit(solution)/shard_map/reduce_scatter | solution.py:74
  165.4 3.7 fusion.7
  169.2 64.6 %all-gather.3.cloned.1.call-done = bf16[1024,3072]{1,0:T(8,128)(2,1)} async-done(((bf16[64,3072]{1,0:T(8,128)(2,1)}), bf16[1024,3072]{1,0:T(8,128)(2,1)}) %all-gather.3.cloned.1.call-update) | async-done | bytes 6291472 | tf_op jit(solution)/shard_map/all_gather | solution.py:80
  233.8 6.4 convolution_convert_fusion.2
  240.3 30.5 %reduce-scatter.6.cloned.1.call-done = bf16[128,384]{1,0:T(8,128)(2,1)} async-done(((bf16[1024,384]{1,0:T(8,128)(2,1)}), bf16[128,384]{1,0:T(8,128)(2,1)}) %reduce-scatter.6.cloned.1.call-update) | async-done | bytes 98320 | tf_op jit(solution)/shard_map/reduce_scatter | solution.py:81
  270.9 1.7 convolution_convert_fusion.4
  272.7 130.9 %all-reduce.6.cloned.1.call-done = bf16[128,256]{1,0:T(8,128)(2,1)} async-done(((bf16[128,256]{1,0:T(8,128)(2,1)}), bf16[128,256]{1,0:T(8,128)(2,1)}) %all-reduce.6.cloned.1.call-update) | async-done | bytes 65552 | tf_op jit(solution)/shard_map/psum | solution.py:88
  403.6 1.8 fusion.48
  406.0 3.1 collective-permute-start
  409.1 1.3 collective-permute-start.1
  411.7 2.4 copy.12
  416.6 16.6 %all-reduce.3 = (f32[]{:T(128)}, f32[]{:T(128)}, f32[]{:T(128)}) all-reduce(f32[]{:T(128)} %get-tuple-element.6, f32[]{:T(128)} %convert_reduce_fusion.1, f32[]{:T(128)} %get-tuple-element.5), channel_id=1, replica_groups=mesh['row'=16,'col'=8] {'col'}, use_global_device_ids=true, to_apply=%region_8.9 | all-reduce | flops 3 | bytes 24 | tf_op jit(solution)/shard_map/psum | solution.py:107
  437.4 3.3 collective-permute-done.3
  446.8 2.6 convolution_convert_fusion.3
  449.4 24.0 %all_gather.14 = bf16[1024,384]{1,0:T(8,128)(2,1)S(1)} all-gather(bf16[128,384]{1,0:T(8,128)(2,1)} %convolution_convert_fusion.3), channel_id=1, replica_groups=mesh['row'=16,'col'=8] {'col'}, dimensions={0}, use_global_device_ids=true | all-gather | bytes 884736 | tf_op jit(solution)/shard_map/all_gather | solution.py:123
  474.3 5.4 convolution_convert_fusion
  480.0 101.9 %reduce-scatter.8.cloned.1.call-done = bf16[64,3072]{1,0:T(8,128)(2,1)} async-done(((bf16[1024,3072]{1,0:T(8,128)(2,1)}), bf16[64,3072]{1,0:T(8,128)(2,1)}) %reduce-scatter.8.cloned.1.call-update) | async-done | bytes 393232 | tf_op jit(solution)/shard_map/reduce_scatter | solution.py:128
  581.9 2.4 fusion.42
  585.6 8.6 %fusion.101 = f32[3072,384]{1,0:T(8,128)} fusion(bf16[1024,3072]{1,0:T(8,128)(2,1)} %all-gather.3.cloned.1.call-done, bf16[1024,384]{1,0:T(8,128)(2,1)} %copy-done.4), kind=kOutput, calls=%fused_computation.155 | convolution fusion | flops 2415919104 | bytes 11796480 | tf_op jit(solution)/shard_map/dot_general | solution.py:124
  594.2 54.8 %all-gather.5.cloned.1.call-done = bf16[1024,3072]{1,0:T(8,128)(2,1)} async-done(((bf16[64,3072]{1,0:T(8,128)(2,1)}), bf16[1024,3072]{1,0:T(8,128)(2,1)}) %all-gather.5.cloned.1.call-update) | async-done | bytes 6291472 | tf_op jit(solution)/shard_map/all_gather | solution.py:134
  649.0 7.8 %fusion.92 = f32[384,3072]{1,0:T(8,128)} fusion(bf16[1024,3072]{1,0:T(8,128)(2,1)} %all-gather.5.cloned.1.call-done, bf16[1024,384]{1,0:T(8,128)(2,1)S(1)} %all_gather.12, f32[384]{0:T(512)S(1)} %copy-done.8, f32[1024]{0:T(1024)S(1)} %get-tuple-element.37, f32[1024]{0:T(1024)S(1)} %get-tuple-element.36), kind=kOutput, calls=%fused_computation.151 | convolution fusion | flops 2417885184 | bytes 11806208 | tf_op jit(solution)/shard_map/dot_general | solution.py:137
  (80 shorter events, 15.1 us)
Async XLA Ops:
  7.2 226.6 %copy-start = (bf16[3072,384]{1,0:T(8,128)(2,1)S(1)}, bf16[3072,384]{1,0:T(8,128)(2,1)}, u32[]{:S(2)}) copy-start(bf16[3072,384]{1,0:T(8,128)(2,1)} %param.12) | copy-start | bytes 7077892
  7.2 158.2 %reduce-scatter.4.cloned.1.call-start = ((), (), s32[]{:S(2)}) async-start(), calls=%async_computation.3 | async-start | bytes 6684672 | tf_op jit(solution)/shard_map/reduce_scatter | solution.py:74
  81.0 152.8 %all-gather.3.cloned.1.call-start = ((), (), s32[]{:S(2)}) async-start(), calls=%async_computation.4 | async-start | bytes 6684672 | tf_op jit(solution)/shard_map/all_gather | solution.py:80
  169.1 101.7 %copy-start.3 = (bf16[384,256]{1,0:T(8,128)(2,1)S(1)}, bf16[384,256]{1,0:T(8,128)(2,1)}, u32[]{:S(2)}) copy-start(bf16[384,256]{1,0:T(8,128)(2,1)} %param.13) | copy-start | bytes 589828
  169.1 101.7 %copy-start.6 = (bf16[128,384]{1,0:T(8,128)(2,1)S(1)}, bf16[128,384]{1,0:T(8,128)(2,1)}, u32[]{:S(2)}) copy-start(bf16[128,384]{1,0:T(8,128)(2,1)} %param.9) | copy-start | bytes 294916
  169.2 103.5 %copy-start.9 = (s32[2,64]{1,0:T(2,128)S(1)}, s32[2,64]{1,0:T(2,128)}, u32[]{:S(2)}) copy-start(s32[2,64]{1,0:T(2,128)} %param.16) | copy-start | bytes 1540
  169.2 241.2 %copy-start.10 = (s32[2,64]{1,0:T(2,128)S(1)}, s32[2,64]{1,0:T(2,128)}, u32[]{:S(2)}) copy-start(s32[2,64]{1,0:T(2,128)} %param.17) | copy-start | bytes 1540
  169.2 101.7 %reduce-scatter.6.cloned.1.call-start = ((), (), s32[]{:S(2)}) async-start(), calls=%async_computation.5 | async-start | bytes 884736 | tf_op jit(solution)/shard_map/reduce_scatter | solution.py:81
  240.3 163.3 %all-reduce.6.cloned.1.call-start = ((), (), s32[]{:S(2)}) async-start(), calls=%async_computation.6 | async-start | bytes 131072 | tf_op jit(solution)/shard_map/psum | solution.py:88
  272.6 309.3 %reduce-scatter.8.cloned.1.call-start = ((), (), s32[]{:S(2)}) async-start(), calls=%async_computation.7 | async-start | bytes 6684672 | tf_op jit(solution)/shard_map/reduce_scatter | solution.py:128
  406.0 8.1 %collective-permute-start = (bf16[1,64,256]{2,1,0:T(8,128)(2,1)}, bf16[1,64,256]{2,1,0:T(8,128)(2,1)S(1)}, u32[]{:S(2)}, u32[]{:S(2)}) collective-permute-start(bf16[1,64,256]{2,1,0:T(8,128)(2,1)} %get-tuple-element.34), channel_id=1, source_target_pairs={{0,1},{1,2},{2,3},{3,4},{4,5},{5,6},{6,7},{8,9},{9,10},{10,11},{11... | collective-permute-start | bytes 98312 | tf_op jit(solution)/shard_map/ppermute | solution.py:22
  409.1 5.0 collective-permute-start.1
  411.7 2.7 copy-start.5
  414.1 1.3 copy-start.1
  414.1 1.6 copy-start.7
  414.1 1.6 copy-start.11
  434.7 2.7 collective-permute-start.2
  436.0 4.7 collective-permute-start.3
  473.4 1.0 copy-start.4
  479.7 102.2 %copy-start.2 = (bf16[64,3072]{1,0:T(8,128)(2,1)S(1)}, bf16[64,3072]{1,0:T(8,128)(2,1)}, u32[]{:S(2)}) copy-start(bf16[64,3072]{1,0:T(8,128)(2,1)} %reduce-scatter.4.cloned.1.call-done) | copy-start | bytes 1179652
  479.8 169.3 %all-gather.5.cloned.1.call-start = ((), (), s32[]{:S(2)}) async-start(), calls=%async_computation.8 | async-start | bytes 6684672 | tf_op jit(solution)/shard_map/all_gather | solution.py:134
  585.6 63.4 %copy-start.8 = (f32[384]{0:T(512)S(1)}, f32[384]{0:T(512)}, u32[]{:S(2)}) copy-start(f32[384]{0:T(512)} %param.10) | copy-start | bytes 4612
Sparse Core Ops, SparseCore 0:
  81.2 84.2 reduce-scatter.3
  169.3 64.5 all-gather.2
  240.4 30.4 reduce-scatter.5
  273.8 129.8 all-reduce.5
  479.9 101.9 reduce-scatter.7
  584.4 64.5 all-gather.4
where the time goes:
time: 665 us
  waiting for transfers between devices  470 us (71%)
  blocking collectives  107 us (16%)
  matrix products  41.1 us (6%)
  between operations  18.2 us (3%)
  local copies, waits for them, and re-layouts  11.2 us (2%)
  other arithmetic  9.85 us (1%)
  starting transfers between devices  7.39 us (1%)
    psum x1, waiting for transfers between devices, on_device(): lax.psum(jnp.dot(mixed, proj, preferred_element_type=jnp.float32).astype(...  131 us
    reduce_scatter x1, waiting for transfers between devices, on_device(): lax.psum_scatter(back_term(jnp.int32(0), lax.axis_size('row') * (total //...  102 us
    reduce_scatter x1, waiting for transfers between devices, on_device(): lax.psum_scatter(jnp.dot(normed, w_up, preferred_element_type=jnp.float32...  84.3 us
    all_gather x1, waiting for transfers between devices, on_device(): lax.all_gather(gelu_exact(pre_share).astype(jnp.bfloat16), 'row', axis=0,...  64.6 us
    all_gather x1, waiting for transfers between devices, on_device(): lax.all_gather(gelu_back(pre_share, back_share).astype(jnp.bfloat16), 'ro...  54.8 us
    psum x1, blocking collectives, on_device(): lax.psum((jnp.sum(xf_all, 1), jnp.sum(xf_all * xf_all, 1)), 'row')  40.2 us
    reduce_scatter x1, waiting for transfers between devices, on_device(): lax.psum_scatter(jnp.dot(hidden, w_down, preferred_element_type=jnp.float...  30.5 us
    all_gather x1, blocking collectives, on_device(): rows_all = lax.all_gather(tokens, 'col', axis=0, tiled=True)  25.9 us
  transfers between devices with their start and end apart: 10, of which 7 were waited for; matrix products, arithmetic and copies ran while one was open for 2% of the time, Pallas kernels for 0%

commit v1 on v0

v1 whole, which is shorter than its diff:
```python
import math

import jax
import jax.numpy as jnp
from jax import lax
from jax.experimental import pallas as pl
from jax.experimental.pallas import tpu as pltpu
from jax.sharding import PartitionSpec as P

MESH = pl.DeviceIdType.MESH
F32 = jnp.float32
BF16 = jnp.bfloat16

WIDTH = 6144
GW = 64
GH = 16
TOK = 1024
STRIP = 128
FEAT = 384
HID = 3072
HALF = 1536
OWN = 192
CH = 256
TA = 512
TB = TOK - TA
GA = TA + CH
FOCUS = 0.85
EPS = 1e-06

ROOT_HALF = math.sqrt(0.5)
DENSITY = 1.0 / math.sqrt(2.0 * math.pi)

N_SEMS = 192


def cdf(v):
    return 0.5 * (1.0 + lax.erf(v * ROOT_HALF))


def slope(v):
    return cdf(v) + v * (DENSITY * jnp.exp(-0.5 * v * v))


def tn(a, b):
    return lax.dot_general(a, b, (((0,), (0,)), ((), ())), preferred_element_type=F32)


def nt(a, b):
    return lax.dot_general(a, b, (((1,), (1,)), ((), ())), preferred_element_type=F32)


def mm(a, b):
    return jnp.dot(a, b, preferred_element_type=F32)


def step_kernel(
    tok_ref, gain_ref, wup_ref, wdn_hbm, proj_ref, conv_hbm, head_ref, depth_ref, mask_ref,
    nt_out, ga_out, gb_out, loss_ref,
    wdn, conv, xall, st_row, st_col, w_t, w_send, wd_peer, proj_peer, n_t, m_part, m_recv, m_own,
    p_a, p_b, a1, a2, a3, b1, b2, b3, pre, hid, der, zc, z1, z1_recv, z2, z2_recv, z3,
    pred_all, rows_buf, gz, ga_own, gb_own, send_sems, recv_sems, local_sems,
):
    row, col = lax.axis_index("row"), lax.axis_index("col")
    z, h, c = row // 4, lax.rem(row // 2, 2), lax.rem(row, 2)
    used = [0]

    def zz(dz):
        return lax.rem(z + dz + 4, 4)

    def hh(dh):
        return lax.rem(h + dh, 2)

    def at_row(dz, dh, dc):
        return {"row": zz(dz) * 4 + hh(dh) * 2 + lax.rem(c + dc, 2)}

    def at_col(dl, dx):
        return {"col": lax.rem(col // 4 + dl, 2) * 4 + lax.rem(lax.rem(col, 4) + dx, 4)}

    def remote(src, dst, device):
        at = used[0]
        used[0] += 1
        copy = pltpu.make_async_remote_copy(
            src_ref=src, dst_ref=dst, send_sem=send_sems.at[at], recv_sem=recv_sems.at[at],
            device_id=device, device_id_type=MESH,
        )
        copy.start()
        sent.append(copy)
        return copy

    sent = []
    row_peers = [
        (dz, dh, dc) for dz in (2, 1, 3, 0) for dh in (1, 0) for dc in (1, 0) if (dz, dh, dc) != (0, 0, 0)
    ]
    chip_peers = [(dz, dh) for dz in (2, 1, 3, 0) for dh in (1, 0) if (dz, dh) != (0, 0)]
    col_peers = [(dl, dx) for dl in (1, 0) for dx in (2, 1, 3, 0) if (dl, dx) != (0, 0)]
    partner = at_row(0, 0, 1)
    here = z * 2 + h
    other = 1 - c

    barrier = pltpu.get_barrier_semaphore()
    for peer in row_peers:
        pl.semaphore_signal(barrier, inc=1, device_id=at_row(*peer), device_id_type=MESH)
    for peer in col_peers:
        pl.semaphore_signal(barrier, inc=1, device_id=at_col(*peer), device_id_type=MESH)

    wdn_copy = pltpu.make_async_copy(wdn_hbm, wdn, local_sems.at[0])
    wdn_copy.start()
    first_channel = pl.multiple_of(c * 128 + here * 16, 16)
    conv_copy = pltpu.make_async_copy(
        conv_hbm.at[:, pl.ds(first_channel, 16), :], conv, local_sems.at[1]
    )
    conv_copy.start()

    x_t = tok_ref[...].astype(F32).T
    xall[col] = x_t.astype(BF16)
    st_row[row] = jnp.concatenate(
        [
            jnp.sum(x_t, 0, keepdims=True),
            jnp.sum(x_t * x_t, 0, keepdims=True),
            jnp.zeros((6, STRIP), F32),
        ],
        axis=0,
    )
    pl.semaphore_wait(barrier, len(row_peers) + len(col_peers))

    stat_copies = [remote(st_row.at[row], st_row.at[row], at_row(*peer)) for peer in row_peers]
    token_copies = [remote(xall.at[col], xall.at[col], at_col(*peer)) for peer in col_peers]
    wdn_copy.wait()
    to_peer = pl.multiple_of(other * HALF, HALF)
    wd_copy = remote(wdn.at[pl.ds(to_peer, HALF)], wd_peer, partner)
    proj_copy = remote(proj_ref, proj_peer, partner)

    feature_at = pl.multiple_of(c * FEAT, 128)

    @pl.loop(0, HALF // 128)
    def _(i):
        at = pl.multiple_of(to_peer + i * 128, 128)
        w_send[pl.ds(pl.multiple_of(i * 128, 128), 128), :] = wup_ref[:, pl.ds(at, 128)].T

    w_copy = remote(w_send, w_t.at[:, pl.ds(feature_at, FEAT)], partner)

    for copy in stat_copies:
        copy.wait_recv()
    total = st_row[0]
    for index in range(1, 16):
        total = total + st_row[index]
    mean = total[0:1] / WIDTH
    spread = total[1:2] / WIDTH - mean * mean
    depth = depth_ref[...].astype(F32)
    seen = mask_ref[...].astype(F32)
    st_col[col] = jnp.concatenate(
        [
            mean,
            lax.rsqrt(spread + EPS),
            jnp.concatenate([seen[0:1], seen[1:2]], axis=1),
            jnp.log(jnp.concatenate([depth[0:1], depth[1:2]], axis=1) * 0.001),
            jnp.zeros((4, STRIP), F32),
        ],
        axis=0,
    )
    norm_copies = [remote(st_col.at[col], st_col.at[col], at_col(*peer)) for peer in col_peers]

    own_half = pl.multiple_of(c * HALF, HALF)

    @pl.loop(0, HALF // 128)
    def _(i):
        at = pl.multiple_of(own_half + i * 128, 128)
        w_t[pl.ds(pl.multiple_of(i * 128, 128), 128), pl.ds(feature_at, FEAT)] = wup_ref[:, pl.ds(at, 128)].T

    wd_copy.wait_recv()
    proj_copy.wait_recv()

    @pl.loop(0, 8)
    def _(k):
        at = pl.multiple_of(k * OWN, 64)
        m_part[k] = (
            mm(wdn[pl.ds(own_half + at, OWN), :], proj_ref[...]) + mm(wd_peer[pl.ds(at, OWN), :], proj_peer[...])
        ).astype(BF16)

    m_copies = []
    for index, (dz, dh) in enumerate(chip_peers):
        m_copies.append(
            remote(m_part.at[zz(dz) * 2 + hh(dh)], m_recv.at[index], at_row(dz, dh, 0))
        )

    gain = jnp.broadcast_to(gain_ref[...], (STRIP, FEAT)).T
    for copy in norm_copies:
        copy.wait_recv()
    for copy in token_copies:
        copy.wait_recv()

    for index in range(8):
        stats = st_col[index]
        n_t[pl.ds(feature_at, FEAT), index * STRIP : (index + 1) * STRIP] = (
            (xall[index].astype(F32) - stats[0:1]) * stats[1:2] * gain
        ).astype(BF16)
    n_own = n_t.at[pl.ds(feature_at, FEAT)]
    n_copy = remote(n_own, n_own, partner)
    n_out_copy = pltpu.make_async_copy(n_own, nt_out, local_sems.at[2])
    n_out_copy.start()
    w_copy.wait_recv()
    n_copy.wait_recv()

    a_copies, b_copies = {}, {}

    def project(dz):
        base = pl.multiple_of(zz(dz) * 2 * OWN, 2 * OWN)

        @pl.loop(0, TOK // 256)
        def _(t):
            at = pl.multiple_of(t * 256, 256)
            both = mm(w_t[pl.ds(base, 2 * OWN), :], n_t[:, pl.ds(at, 256)]).astype(BF16)

            @pl.when(t < TA // 256)
            def _():
                p_a[zz(dz), 0, :, pl.ds(at, 256)] = both[:OWN]
                p_a[zz(dz), 1, :, pl.ds(at, 256)] = both[OWN:]

            @pl.when(t >= TA // 256)
            def _():
                at_b = pl.multiple_of(jnp.maximum(at - TA, 0), 256)
                p_b[zz(dz), 0, :, pl.ds(at_b, 256)] = both[:OWN]
                p_b[zz(dz), 1, :, pl.ds(at_b, 256)] = both[OWN:]

    up, down, flip = at_row(1, 0, 0), at_row(3, 0, 0), at_row(0, 1, 0)
    for dz in (2, 1, 3, 0):
        project(dz)
        b_copies[dz] = remote(p_b.at[zz(dz), 1 - h], b1.at[zz(dz)], flip)
        if dz == 2:
            a_up = remote(p_a.at[zz(2), 0], a1.at[0], up)
            a_down = remote(p_a.at[zz(2), 1], a1.at[1], down)

    def add(into, more):
        into[...] = (into[...].astype(F32) + more[...].astype(F32)).astype(BF16)

    a_up.wait_recv()
    add(p_a.at[zz(1), 0], a1.at[0])
    a_up2 = remote(p_a.at[zz(1)], a2.at[0], up)
    a_down.wait_recv()
    add(p_a.at[zz(3), 1], a1.at[1])
    a_down2 = remote(p_a.at[zz(3)], a2.at[1], down)

    b_copies[2].wait_recv()
    add(p_b.at[zz(2), h], b1.at[zz(2)])
    b_up = remote(p_b.at[zz(2), h, 0:96], b2.at[0], up)
    b_down = remote(p_b.at[zz(2), h, 96:192], b2.at[1], down)
    b_copies[1].wait_recv()
    add(p_b.at[zz(1), h], b1.at[zz(1)])
    b_copies[3].wait_recv()
    add(p_b.at[zz(3), h], b1.at[zz(3)])

    a_up2.wait_recv()
    a_down2.wait_recv()
    p_a[z, 1 - h] = (
        p_a[z, 1 - h].astype(F32) + a2[0, 1 - h].astype(F32) + a2[1, 1 - h].astype(F32)
    ).astype(BF16)
    a_flip = remote(p_a.at[z, 1 - h], a3, flip)

    b_up.wait_recv()
    add(p_b.at[zz(1), h, 0:96], b2.at[0])
    b_up2 = remote(p_b.at[zz(1), h], b3.at[0], up)
    b_down.wait_recv()
    add(p_b.at[zz(3), h, 96:192], b2.at[1])
    b_down2 = remote(p_b.at[zz(3), h], b3.at[1], down)

    for copy in m_copies:
        copy.wait_recv()
    m_sum = m_part[here].astype(F32)
    for index in range(7):
        m_sum = m_sum + m_recv[index].astype(F32)
    m_own[...] = m_sum.astype(BF16)
    x_proj = tn(proj_ref[...], xall[col])

    conv_copy.wait()
    head = head_ref[...]
    taps = [jnp.sum(conv[k].astype(F32) * head, axis=1, keepdims=True) for k in range(9)]
    lane = lax.broadcasted_iota(jnp.int32, (16, CH), 1)
    sub = lax.broadcasted_iota(jnp.int32, (16, CH), 0)
    head_col = jnp.sum(jnp.where(lane == sub + first_channel, head, 0.0), axis=1, keepdims=True)

    b_copies[0].wait_recv()
    a_flip.wait_recv()
    pre[:, :TA] = (
        p_a[z, h].astype(F32) + a2[0, h].astype(F32) + a2[1, h].astype(F32) + a3[...].astype(F32)
    )
    b_up2.wait_recv()
    b_down2.wait_recv()
    pre[:, TA:] = (
        p_b[z, h].astype(F32) + b1[z].astype(F32) + b3[0].astype(F32) + b3[1].astype(F32)
    )

    @pl.loop(0, TOK // 128)
    def _(t):
        at = pl.ds(pl.multiple_of(t * 128, 128), 128)
        value = pre[:, at]
        hid[:, at] = (value * cdf(value)).astype(BF16)

    @pl.loop(0, TOK // 256)
    def _(t):
        at = pl.ds(pl.multiple_of(t * 256, 256), 256)
        zc[:, at] = tn(m_own[...], hid[:, at])

    strip = pl.ds(pl.multiple_of(col * STRIP, STRIP), STRIP)
    zc[:, strip] = zc[:, strip] + x_proj

    z1[...] = zc[pl.ds(pl.multiple_of(other * 128, 128), 128), :].astype(BF16)
    z1_copy = remote(z1, z1_recv, partner)

    @pl.loop(0, TOK // 128)
    def _(t):
        at = pl.ds(pl.multiple_of(t * 128, 128), 128)
        der[:, at] = slope(pre[:, at])

    z1_copy.wait_recv()
    z2[...] = (
        zc[pl.ds(pl.multiple_of(c * 128, 128), 128), :] + z1_recv[...].astype(F32)
    ).astype(BF16)
    z2_copies = []
    for index, (dz, dh) in enumerate(chip_peers):
        at = pl.multiple_of((zz(dz) * 2 + hh(dh)) * 16, 16)
        z2_copies.append(remote(z2.at[pl.ds(at, 16)], z2_recv.at[index], at_row(dz, dh, 0)))
    part = z2[pl.ds(pl.multiple_of(here * 16, 16), 16), :].astype(F32)
    for index, copy in enumerate(z2_copies):
        copy.wait_recv()
        part = part + z2_recv[index].astype(F32)
    z3[col] = part.astype(BF16)
    z3_copies = [remote(z3.at[col], z3.at[col], at_col(*peer)) for peer in col_peers]
    for copy in z3_copies:
        copy.wait_recv()
    field = z3[0].astype(F32)
    for index in range(1, 8):
        field = field + z3[index].astype(F32)

    token = lax.broadcasted_iota(jnp.int32, (1, TOK), 1)
    line, place = token >> 6, token & (GW - 1)

    def moved(values, di, dj):
        shift = di * GW + dj
        if shift:
            values = pltpu.roll(values, (-shift) % TOK, 1)
        inside = (
            (line + di >= 0) & (line + di < GH) & (place + dj >= 0) & (place + dj < GW)
        )
        return jnp.where(inside, values, 0.0)

    act = (field * cdf(field)).astype(BF16).astype(F32)
    pred = jnp.sum(field * head_col, axis=0, keepdims=True)
    for k in range(9):
        pred = pred + moved(jnp.sum(act * taps[k], axis=0, keepdims=True), k // 3 - 1, k % 3 - 1)
    for index in range(8):
        rows_buf[index : index + 1, :] = pred[:, index * STRIP : (index + 1) * STRIP]
    pred_all[row] = rows_buf[...]
    pred_copies = [remote(pred_all.at[row], pred_all.at[row], at_row(*peer)) for peer in row_peers]
    field_slope = slope(field)
    valid = jnp.concatenate([st_col[index][2:3] for index in range(8)], axis=0)
    target = jnp.concatenate([st_col[index][3:4] for index in range(8)], axis=0)
    for copy in pred_copies:
        copy.wait_recv()
    pred = pred_all[0]
    for index in range(1, 16):
        pred = pred + pred_all[index]

    err = valid * (pred - target)

    def whole(values):
        return jnp.sum(jnp.sum(values, axis=1, keepdims=True), axis=0, keepdims=True)

    count = whole(valid)
    mean_err = whole(err) / count
    loss_ref[...] = jnp.broadcast_to(
        whole(err * err) / count - FOCUS * mean_err * mean_err, loss_ref.shape
    )
    grad_pred = valid * (2.0 * err - 2.0 * FOCUS * mean_err)
    grad_pred = jnp.concatenate([grad_pred[index : index + 1] for index in range(8)], axis=1)
    back = jnp.zeros((16, TOK), F32)
    for k in range(9):
        back = back + taps[k] * moved(grad_pred, 1 - k // 3, 1 - k % 3)
    mine = pl.ds(first_channel, 16)
    gz[mine, :] = (grad_pred * head_col + field_slope * back).astype(BF16)

    gz_copies = [
        remote(gz.at[mine], gz.at[mine], at_row(dz, dh, 0)) for dz, dh in chip_peers
    ]
    gz_pair = [remote(gz.at[mine], gz.at[mine], partner)]
    for (dz, dh), copy in zip(chip_peers, gz_copies):
        copy.wait_recv()
        came = gz.at[pl.ds(pl.multiple_of(c * 128 + (zz(-dz) * 2 + hh(dh)) * 16, 16), 16)]
        gz_pair.append(remote(came, came, partner))
    for copy in gz_pair:
        copy.wait_recv()

    @pl.loop(0, TOK // 256)
    def _(t):
        at = pl.multiple_of(t * 256, 256)
        lanes = pl.ds(at, 256)
        grad = (mm(m_own[...], gz[:, lanes]) * der[:, lanes]).astype(BF16)

        @pl.when(t < TA // 256)
        def _():
            ga_own[:, lanes] = grad

        @pl.when(t >= TA // 256)
        def _():
            gb_own[:, pl.ds(pl.multiple_of(jnp.maximum(at - TA, 0), 256), 256)] = grad

    ga_own[:, TA:] = nt(hid[...], gz[...]).astype(BF16)

    def slot(dz, dh):
        return c * 8 + zz(dz) * 2 + hh(dh)

    mine_a, mine_b = ga_out.at[slot(0, 0)], gb_out.at[slot(0, 0)]
    own_copies = [
        pltpu.make_async_copy(ga_own, mine_a, local_sems.at[3]),
        pltpu.make_async_copy(gb_own, mine_b, local_sems.at[4]),
    ]
    fa = remote(ga_own, mine_a, flip)
    bu = remote(gb_own, mine_b, up)
    bd = remote(gb_own, mine_b, down)
    fb = remote(gb_own, mine_b, flip)
    au = remote(ga_own, mine_a, up)
    ad = remote(ga_own, mine_a, down)
    for copy in own_copies:
        copy.start()
    pair = [remote(ga_own, mine_a, partner), remote(gb_own, mine_b, partner)]

    def send(buf, dz, dh, device, rows=None):
        ref = buf.at[slot(dz, dh)] if rows is None else buf.at[slot(dz, dh), rows[0] : rows[1]]
        return remote(ref, ref, device)

    top, low = (0, 96), (96, 192)
    bu.wait_recv()
    bu2 = send(gb_out, 3, 0, up, top)
    f_m = send(gb_out, 3, 0, flip)
    pair.append(send(gb_out, 3, 0, partner))
    bd.wait_recv()
    bd2 = send(gb_out, 1, 0, down, low)
    f_p = send(gb_out, 1, 0, flip)
    pair.append(send(gb_out, 1, 0, partner))
    fa.wait_recv()
    fau = send(ga_out, 0, 1, up)
    fad = send(ga_out, 0, 1, down)
    pair.append(send(ga_out, 0, 1, partner))
    fb.wait_recv()
    pair.append(send(gb_out, 0, 1, partner))
    bu2.wait_recv()
    f_top = send(gb_out, 2, 0, flip, top)
    pair.append(send(gb_out, 2, 0, partner, top))
    bd2.wait_recv()
    f_low = send(gb_out, 2, 0, flip, low)
    pair.append(send(gb_out, 2, 0, partner, low))
    au.wait_recv()
    au2 = send(ga_out, 3, 0, up)
    pair.append(send(ga_out, 3, 0, partner))
    ad.wait_recv()
    pair.append(send(ga_out, 1, 0, partner))
    f_m.wait_recv()
    pair.append(send(gb_out, 3, 1, partner))
    fad.wait_recv()
    fad2 = send(ga_out, 1, 1, down)
    pair.append(send(ga_out, 1, 1, partner))
    fau.wait_recv()
    pair.append(send(ga_out, 3, 1, partner))
    f_p.wait_recv()
    pair.append(send(gb_out, 1, 1, partner))
    f_top.wait_recv()
    pair.append(send(gb_out, 2, 1, partner, top))
    f_low.wait_recv()
    pair.append(send(gb_out, 2, 1, partner, low))
    au2.wait_recv()
    pair.append(send(ga_out, 2, 0, partner))
    fad2.wait_recv()
    pair.append(send(ga_out, 2, 1, partner))
    for copy in pair:
        copy.wait_recv()
    for copy in own_copies:
        copy.wait()
    n_out_copy.wait()
    for copy in sent:
        copy.wait_send()


def weight_kernel(n_ref, ga_ref, gb_ref, proj_ref, up_ref, down_ref):
    part_a = ga_ref[...].reshape(2 * OWN, GA)
    part_b = gb_ref[...].reshape(2 * OWN, TB)
    up_ref[...] = nt(n_ref[:, :TA], part_a[:, :TA]) + nt(n_ref[:, TA:], part_b)
    down_ref[...] = nt(part_a[:, TA:], proj_ref[...])


def on_device(tokens, ln_gain, w_up, w_down, proj, conv_kernel, head_weight, depth_mm, lidar_mask):
    vmem = pl.BlockSpec(memory_space=pltpu.VMEM)
    anywhere = pl.BlockSpec(memory_space=pl.ANY)
    normed, grads_a, grads_b, loss = pl.pallas_call(
        step_kernel,
        name="mlp_step",
        out_shape=[
            jax.ShapeDtypeStruct((FEAT, TOK), BF16),
            jax.ShapeDtypeStruct((16, OWN, GA), BF16),
            jax.ShapeDtypeStruct((16, OWN, TB), BF16),
            jax.ShapeDtypeStruct((8, 128), F32),
        ],
        in_specs=[vmem, vmem, vmem, anywhere, vmem, anywhere, vmem, vmem, vmem],
        out_specs=[anywhere, anywhere, anywhere, vmem],
        scratch_shapes=[
            pltpu.VMEM((HID, FEAT), BF16),
            pltpu.VMEM((9, 16, CH), BF16),
            pltpu.VMEM((8, FEAT, STRIP), BF16),
            pltpu.VMEM((16, 8, STRIP), F32),
            pltpu.VMEM((8, 8, STRIP), F32),
            pltpu.VMEM((HALF, 2 * FEAT), BF16),
            pltpu.VMEM((HALF, FEAT), BF16),
            pltpu.VMEM((HALF, FEAT), BF16),
            pltpu.VMEM((FEAT, CH), BF16),
            pltpu.VMEM((2 * FEAT, TOK), BF16),
            pltpu.VMEM((8, OWN, CH), BF16),
            pltpu.VMEM((7, OWN, CH), BF16),
            pltpu.VMEM((OWN, CH), BF16),
            pltpu.VMEM((4, 2, OWN, TA), BF16),
            pltpu.VMEM((4, 2, OWN, TB), BF16),
            pltpu.VMEM((2, OWN, TA), BF16),
            pltpu.VMEM((2, 2, OWN, TA), BF16),
            pltpu.VMEM((OWN, TA), BF16),
            pltpu.VMEM((4, OWN, TB), BF16),
            pltpu.VMEM((2, OWN // 2, TB), BF16),
            pltpu.VMEM((2, OWN, TB), BF16),
            pltpu.VMEM((OWN, TOK), F32),
            pltpu.VMEM((OWN, TOK), BF16),
            pltpu.VMEM((OWN, TOK), F32),
            pltpu.VMEM((CH, TOK), F32),
            pltpu.VMEM((128, TOK), BF16),
            pltpu.VMEM((128, TOK), BF16),
            pltpu.VMEM((128, TOK), BF16),
            pltpu.VMEM((7, 16, TOK), BF16),
            pltpu.VMEM((8, 16, TOK), BF16),
            pltpu.VMEM((16, 8, STRIP), F32),
            pltpu.VMEM((8, STRIP), F32),
            pltpu.VMEM((CH, TOK), BF16),
            pltpu.VMEM((OWN, GA), BF16),
            pltpu.VMEM((OWN, TB), BF16),
            pltpu.SemaphoreType.DMA((N_SEMS,)),
            pltpu.SemaphoreType.DMA((N_SEMS,)),
            pltpu.SemaphoreType.DMA((5,)),
        ],
        compiler_params=pltpu.CompilerParams(
            collective_id=0, has_side_effects=True, vmem_limit_bytes=50 * 2**20
        ),
        cost_estimate=pl.CostEstimate(flops=4 * 10**9, bytes_accessed=16 * 2**20, transcendentals=10**6),
    )(
        tokens,
        ln_gain.reshape(1, FEAT),
        w_up,
        w_down,
        proj,
        conv_kernel.reshape(9, CH, CH),
        head_weight.reshape(1, CH),
        depth_mm,
        lidar_mask,
    )
    grad_up, grad_down = pl.pallas_call(
        weight_kernel,
        name="weight_grads",
        grid=(8,),
        out_shape=[
            jax.ShapeDtypeStruct((FEAT, HID), F32),
            jax.ShapeDtypeStruct((HID, FEAT), F32),
        ],
        in_specs=[
            pl.BlockSpec((FEAT, TOK), lambda j: (0, 0)),
            pl.BlockSpec((2, OWN, GA), lambda j: (j, 0, 0)),
            pl.BlockSpec((2, OWN, TB), lambda j: (j, 0, 0)),
            pl.BlockSpec((FEAT, CH), lambda j: (0, 0)),
        ],
        out_specs=[
            pl.BlockSpec((FEAT, 2 * OWN), lambda j: (0, j)),
            pl.BlockSpec((2 * OWN, FEAT), lambda j: (j, 0)),
        ],
        compiler_params=pltpu.CompilerParams(vmem_limit_bytes=32 * 2**20),
        cost_estimate=pl.CostEstimate(flops=3 * 10**9, bytes_accessed=18 * 2**20, transcendentals=0),
    )(normed, grads_a, grads_b, proj)
    return (grad_up, grad_down, loss[0, 0])


def solution(mesh):
    return jax.shard_map(
        on_device,
        mesh=mesh,
        in_specs=(
            P("col", "row"),
            P("row"),
            P("row", "col"),
            P("col", "row"),
            P("row", None),
            P(),
            P(),
            P("col", None),
            P("col", None),
        ),
        out_specs=(P("row", "col"), P("col", "row"), P()),
        check_vma=False,
    )
```

time: 665 us -> 137 us (0.21)
  waiting for transfers between devices: 470 us -> 0 us
  Pallas kernels: 0 us -> 126 us
  blocking collectives: 107 us -> 0 us
  matrix products: 41.1 us -> 0 us
  between operations: 18.2 us -> 0.65 us
  other arithmetic: 9.85 us -> 0 us
  starting transfers between devices: 7.39 us -> 0 us
    reduce_scatter x3 -> x0, waiting for transfers between devices: 217 us -> none  [the longest x1 102 us: on_device(): lax.psum_scatter(back_term(jnp.int32(0), lax.axis_size('row') * (total //...]
    psum x1 -> x0, waiting for transfers between devices: 131 us -> none  [on_device(): lax.psum(jnp.dot(mixed, proj, preferred_element_type=jnp.float32).astype(...]
    pallas_call x0 -> x2, Pallas kernels: none -> 126 us  [the longest x1 119 us: on_device(): pl.pallas_call(step_kernel, name='mlp_step', out_shape=[jax.ShapeDtypeStr...]
    all_gather x2 -> x0, waiting for transfers between devices: 119 us -> none  [the longest x1 64.6 us: on_device(): lax.all_gather(gelu_exact(pre_share).astype(jnp.bfloat16), 'row', axis=0,...]
    psum x2 -> x0, blocking collectives: 56.8 us -> none  [the longest x1 40.2 us: on_device(): lax.psum((jnp.sum(xf_all, 1), jnp.sum(xf_all * xf_all, 1)), 'row')]
    all_gather x2 -> x0, blocking collectives: 49.8 us -> none  [the longest x1 25.9 us: on_device(): rows_all = lax.all_gather(tokens, 'col', axis=0, tiled=True)]
    dot_general x9 -> x0, matrix products: 41.1 us -> none  [the longest x1 8.62 us: on_device(): lax.dot_general(hidden, grad_rows, (((0,), (0,)), ((), ())), preferred_el...]
    convert_element_type x6 -> x0, other arithmetic: 8.01 us -> none  [the longest x1 3.69 us: on_device(): gelu_exact(pre_share).astype(jnp.bfloat16)]
  transfers between devices with their start and end apart: 10 -> 0, of which waited for: 7 -> 0; matrix products, arithmetic and copies ran while one was open for 2% -> 0% of each run, Pallas kernels for 0% -> 0%
where the time goes in v1:
time: 137 us
  Pallas kernels  126 us (92%)
  local copies, waits for them, and re-layouts  10.5 us (8%)
    pallas_call x1, Pallas kernels, on_device(): pl.pallas_call(step_kernel, name='mlp_step', out_shape=[jax.ShapeDtypeStr...  119 us
    unnamed x16, local copies, waits for them, and re-layouts  9.35 us
    pallas_call x1, Pallas kernels, on_device(): pl.pallas_call(weight_kernel, name='weight_grads', grid=(8,), out_shape=[...  7.09 us

profile of v1, /device:TPU:1, one launch (start us, length us, event | category | flops | bytes accessed | tf_op | source)
XLA Modules:
  0.0 137.0 jit_solution(2235766442580055981)
XLA Ops:
  0.6 0.7 reshape.15.gain_ref
  1.3 0.0 copy-start
  1.3 1.3 copy-done
  2.6 0.0 copy-start.1
  2.6 0.9 copy-done.1
  3.5 0.0 copy-start.2
  3.5 0.9 copy-done.2
  4.4 0.0 copy-start.3
  4.4 0.7 copy-done.3
  5.1 0.0 copy-start.4
  5.1 0.7 copy-done.4
  5.8 0.0 copy-start.5
  5.8 0.7 copy-done.5
  6.4 118.7 %mlp_step.1 = (bf16[384,1024]{1,0:T(8,128)(2,1)S(1)}, bf16[16,192,768]{2,1,0:T(8,128)(2,1)}, bf16[16,192,512]{2,1,0:T(8,128)(2,1)}, f32[8,128]{1,0:T(8,128)S(1)}) custom-call(bf16[128,384]{1,0:T(8,128)(2,1)S(1)} %copy-done.2, f32[1,384]{1,0:T(1,128)S(1)} %reshape.15.gain_ref, bf16[384,3072]{1,0:T(8,128)(2,1)} %wup_ref.1, bf16[3072,384]{1,0:T(8,128)(2,1)} %wdn_hbm.1, ...), custom_call_target="tpu_custom_call" | custom-call | flops 4000000000 | bytes 16777216 | tf_op jit(solution)/shard_map/mlp_step/pallas_call | solution.py:492
  125.2 0.5 slice.3
  125.7 0.0 copy-start.6
  125.7 2.3 %copy-done.6 = bf16[16,192,768]{2,1,0:T(8,128)(2,1)S(1)} copy-done((bf16[16,192,768]{2,1,0:T(8,128)(2,1)S(1)}, bf16[16,192,768]{2,1,0:T(8,128)(2,1)}, u32[]{:S(2)}) %copy-start.6) | copy-done | bytes 4718616
  128.0 0.0 copy-start.7
  128.0 1.9 %copy-done.7 = bf16[16,192,512]{2,1,0:T(8,128)(2,1)S(1)} copy-done((bf16[16,192,512]{2,1,0:T(8,128)(2,1)S(1)}, bf16[16,192,512]{2,1,0:T(8,128)(2,1)}, u32[]{:S(2)}) %copy-start.7) | copy-done | bytes 3145752
  129.9 7.1 %weight_grads.1 = (f32[384,3072]{1,0:T(8,128)}, f32[3072,384]{1,0:T(8,128)}) custom-call(bf16[384,1024]{1,0:T(8,128)(2,1)S(1)} %get-tuple-element.9.n_ref, bf16[16,192,768]{2,1,0:T(8,128)(2,1)S(1)} %copy-done.6, bf16[16,192,512]{2,1,0:T(8,128)(2,1)S(1)} %copy-done.7, bf16[384,256]{1,0:T(8,128)(2,1)S(1)} %copy-done.1), custom_call_target="tpu_custom_call" | custom-call | flops 3000000000 | bytes 18874368 | tf_op jit(solution)/shard_map/weight_grads/pallas_call | solution.py:558
Async XLA Ops:
  1.3 1.3 copy-start
  2.6 0.9 copy-start.1
  3.5 0.9 copy-start.2
  4.4 0.7 copy-start.3
  5.1 0.7 copy-start.4
  5.8 0.7 copy-start.5
  125.7 2.3 %copy-start.6 = (bf16[16,192,768]{2,1,0:T(8,128)(2,1)S(1)}, bf16[16,192,768]{2,1,0:T(8,128)(2,1)}, u32[]{:S(2)}) copy-start(bf16[16,192,768]{2,1,0:T(8,128)(2,1)} %get-tuple-element.10.ga_ref) | copy-start | bytes 14155780
  128.0 1.9 %copy-start.7 = (bf16[16,192,512]{2,1,0:T(8,128)(2,1)S(1)}, bf16[16,192,512]{2,1,0:T(8,128)(2,1)}, u32[]{:S(2)}) copy-start(bf16[16,192,512]{2,1,0:T(8,128)(2,1)} %get-tuple-element.11.gb_ref) | copy-start | bytes 9437188

commit v2 on v1

v2 whole, which is shorter than its diff:
```python
import math

import jax
import jax.numpy as jnp
from jax import lax
from jax.experimental import pallas as pl
from jax.experimental.pallas import tpu as pltpu
from jax.sharding import PartitionSpec as P

MESH = pl.DeviceIdType.MESH
F32 = jnp.float32
BF16 = jnp.bfloat16

WIDTH = 6144
GW = 64
GH = 16
TOK = 1024
STRIP = 128
FEAT = 384
HID = 3072
HALF = 1536
OWN = 192
CH = 256
TA = 512
TB = TOK - TA
GA = TA + CH
FOCUS = 0.85
EPS = 1e-06

ROOT_HALF = math.sqrt(0.5)
DENSITY = 1.0 / math.sqrt(2.0 * math.pi)

N_SEMS = 192


def cdf(v):
    return 0.5 * (1.0 + lax.erf(v * ROOT_HALF))


def slope(v):
    return cdf(v) + v * (DENSITY * jnp.exp(-0.5 * v * v))


def tn(a, b):
    return lax.dot_general(a, b, (((0,), (0,)), ((), ())), preferred_element_type=F32)


def nt(a, b):
    return lax.dot_general(a, b, (((1,), (1,)), ((), ())), preferred_element_type=F32)


def mm(a, b):
    return jnp.dot(a, b, preferred_element_type=F32)


def step_kernel(
    tok_hbm, gain_ref, wup_hbm, wdn_hbm, proj_hbm, conv_hbm, head_ref, depth_hbm, mask_hbm,
    nt_out, gp_out, gh_out, loss_ref,
    tok_ref, wup_ref, wdn, proj_ref, conv, depth_ref, mask_ref,
    xall, st_row, st_col, w_t, w_send, wd_peer, proj_peer, n_t, m_sum, m_part, m_recv, m_own,
    p_a, p_b, a1, a2, a3, b1, b2, b3, pre, hid, zc, z1, z1_recv, z2, z2_recv, z3,
    pred_all, rows_buf, gz, ga, gb, gh_own, send_sems, recv_sems, local_sems, out_sems,
):
    row, col = lax.axis_index("row"), lax.axis_index("col")
    z, h, c = row // 4, lax.rem(row // 2, 2), lax.rem(row, 2)
    used = [0]

    def zz(dz):
        return lax.rem(z + dz + 4, 4)

    def hh(dh):
        return lax.rem(h + dh, 2)

    def at_row(dz, dh, dc):
        return {"row": zz(dz) * 4 + hh(dh) * 2 + lax.rem(c + dc, 2)}

    def at_col(dl, dx):
        return {"col": lax.rem(col // 4 + dl, 2) * 4 + lax.rem(lax.rem(col, 4) + dx, 4)}

    def remote(src, dst, device):
        at = used[0]
        used[0] += 1
        copy = pltpu.make_async_remote_copy(
            src_ref=src, dst_ref=dst, send_sem=send_sems.at[at], recv_sem=recv_sems.at[at],
            device_id=device, device_id_type=MESH,
        )
        copy.start()
        sent.append(copy)
        return copy

    def slot(dz, dh):
        return c * 8 + zz(dz) * 2 + hh(dh)

    sent = []
    row_peers = [
        (dz, dh, dc) for dz in (2, 1, 3, 0) for dh in (1, 0) for dc in (1, 0) if (dz, dh, dc) != (0, 0, 0)
    ]
    chip_peers = [(dz, dh) for dz in (2, 1, 3, 0) for dh in (1, 0) if (dz, dh) != (0, 0)]
    col_peers = [(dl, dx) for dl in (1, 0) for dx in (2, 1, 3, 0) if (dl, dx) != (0, 0)]
    partner = at_row(0, 0, 1)
    here = z * 2 + h
    other = 1 - c

    barrier = pltpu.get_barrier_semaphore()
    for peer in row_peers:
        pl.semaphore_signal(barrier, inc=1, device_id=at_row(*peer), device_id_type=MESH)
    for peer in col_peers:
        pl.semaphore_signal(barrier, inc=1, device_id=at_col(*peer), device_id_type=MESH)

    started = []

    def local(src, dst):
        copy = pltpu.make_async_copy(src, dst, local_sems.at[len(started)])
        copy.start()
        started.append(copy)
        return copy

    first_channel = pl.multiple_of(c * 128 + here * 16, 16)
    tok_copy = local(tok_hbm, tok_ref)
    proj_in = local(proj_hbm, proj_ref)
    wdn_copy = local(wdn_hbm, wdn)
    wup_copy = local(wup_hbm, wup_ref)
    depth_copy = local(depth_hbm, depth_ref)
    mask_copy = local(mask_hbm, mask_ref)
    conv_copy = local(conv_hbm.at[:, pl.ds(first_channel, 16), :], conv)

    tok_copy.wait()
    x_t = tok_ref[...].astype(F32).T
    xall[col] = x_t.astype(BF16)
    st_row[row] = jnp.concatenate(
        [
            jnp.sum(x_t, 0, keepdims=True),
            jnp.sum(x_t * x_t, 0, keepdims=True),
            jnp.zeros((6, STRIP), F32),
        ],
        axis=0,
    )
    own_half = pl.multiple_of(c * HALF, HALF)
    to_peer = pl.multiple_of(other * HALF, HALF)
    proj_in.wait()
    wdn_copy.wait()

    @pl.loop(0, 8)
    def _(k):
        m_sum[k] = mm(wdn[pl.ds(pl.multiple_of(own_half + k * OWN, 64), OWN), :], proj_ref[...])

    pl.semaphore_wait(barrier, len(row_peers) + len(col_peers))

    stat_copies = [remote(st_row.at[row], st_row.at[row], at_row(*peer)) for peer in row_peers]
    token_copies = [remote(xall.at[col], xall.at[col], at_col(*peer)) for peer in col_peers]
    wd_copy = remote(wdn.at[pl.ds(to_peer, HALF)], wd_peer, partner)
    proj_copy = remote(proj_ref, proj_peer, partner)

    feature_at = pl.multiple_of(c * FEAT, 128)
    wup_copy.wait()

    @pl.loop(0, HALF // 128)
    def _(i):
        at = pl.multiple_of(to_peer + i * 128, 128)
        w_send[pl.ds(pl.multiple_of(i * 128, 128), 128), :] = wup_ref[:, pl.ds(at, 128)].T

    w_copy = remote(w_send, w_t.at[:, pl.ds(feature_at, FEAT)], partner)

    for copy in stat_copies:
        copy.wait_recv()
    total = st_row[0]
    for index in range(1, 16):
        total = total + st_row[index]
    mean = total[0:1] / WIDTH
    spread = total[1:2] / WIDTH - mean * mean
    depth_copy.wait()
    mask_copy.wait()
    depth = depth_ref[...].astype(F32)
    seen = mask_ref[...].astype(F32)
    st_col[col] = jnp.concatenate(
        [
            mean,
            lax.rsqrt(spread + EPS),
            jnp.concatenate([seen[0:1], seen[1:2]], axis=1),
            jnp.log(jnp.concatenate([depth[0:1], depth[1:2]], axis=1) * 0.001),
            jnp.zeros((4, STRIP), F32),
        ],
        axis=0,
    )
    norm_copies = [remote(st_col.at[col], st_col.at[col], at_col(*peer)) for peer in col_peers]

    wd_copy.wait_recv()
    proj_copy.wait_recv()

    @pl.loop(0, 8)
    def _(k):
        more = mm(wd_peer[pl.ds(pl.multiple_of(k * OWN, 64), OWN), :], proj_peer[...])
        m_part[k] = (m_sum[k] + more).astype(BF16)

    m_copies = []
    for index, (dz, dh) in enumerate(chip_peers):
        m_copies.append(
            remote(m_part.at[zz(dz) * 2 + hh(dh)], m_recv.at[index], at_row(dz, dh, 0))
        )

    @pl.loop(0, HALF // 128)
    def _(i):
        at = pl.multiple_of(own_half + i * 128, 128)
        w_t[pl.ds(pl.multiple_of(i * 128, 128), 128), pl.ds(feature_at, FEAT)] = wup_ref[:, pl.ds(at, 128)].T

    gain = jnp.broadcast_to(gain_ref[...].reshape(1, FEAT), (STRIP, FEAT)).T
    for copy in norm_copies:
        copy.wait_recv()
    for copy in token_copies:
        copy.wait_recv()

    n_copies = []
    for first in (0, 4):
        for index in range(first, first + 4):
            stats = st_col[index]
            n_t[pl.ds(feature_at, FEAT), index * STRIP : (index + 1) * STRIP] = (
                (xall[index].astype(F32) - stats[0:1]) * stats[1:2] * gain
            ).astype(BF16)
        half = n_t.at[pl.ds(feature_at, FEAT), first * STRIP : (first + 4) * STRIP]
        n_copies.append(remote(half, half, partner))
    local(n_t.at[pl.ds(feature_at, FEAT)], nt_out)
    w_copy.wait_recv()

    a_copies, b_copies = {}, {}

    def project(dz, into, first):
        base = pl.multiple_of(zz(dz) * 2 * OWN, 2 * OWN)

        @pl.loop(0, into.shape[3] // 256)
        def _(t):
            at = pl.multiple_of(t * 256, 256)
            both = mm(
                w_t[pl.ds(base, 2 * OWN), :], n_t[:, pl.ds(pl.multiple_of(first + at, 256), 256)]
            ).astype(BF16)
            into[zz(dz), 0, :, pl.ds(at, 256)] = both[:OWN]
            into[zz(dz), 1, :, pl.ds(at, 256)] = both[OWN:]

    up, down, flip = at_row(1, 0, 0), at_row(3, 0, 0), at_row(0, 1, 0)
    n_copies[0].wait_recv()
    project(2, p_a, 0)
    a_up = remote(p_a.at[zz(2), 0], a1.at[0], up)
    a_down = remote(p_a.at[zz(2), 1], a1.at[1], down)
    n_copies[1].wait_recv()
    for dz in (2, 1, 3, 0):
        project(dz, p_b, TA)
        b_copies[dz] = remote(p_b.at[zz(dz), 1 - h], b1.at[zz(dz)], flip)
    for dz in (1, 3, 0):
        project(dz, p_a, 0)

    def add(into, more):
        into[...] = (into[...].astype(F32) + more[...].astype(F32)).astype(BF16)

    a_up.wait_recv()
    add(p_a.at[zz(1), 0], a1.at[0])
    a_up2 = remote(p_a.at[zz(1)], a2.at[0], up)
    a_down.wait_recv()
    add(p_a.at[zz(3), 1], a1.at[1])
    a_down2 = remote(p_a.at[zz(3)], a2.at[1], down)

    b_copies[2].wait_recv()
    add(p_b.at[zz(2), h], b1.at[zz(2)])
    b_up = remote(p_b.at[zz(2), h, 0:96], b2.at[0], up)
    b_down = remote(p_b.at[zz(2), h, 96:192], b2.at[1], down)
    b_copies[1].wait_recv()
    add(p_b.at[zz(1), h], b1.at[zz(1)])
    b_copies[3].wait_recv()
    add(p_b.at[zz(3), h], b1.at[zz(3)])

    a_up2.wait_recv()
    a_down2.wait_recv()
    p_a[z, 1 - h] = (
        p_a[z, 1 - h].astype(F32) + a2[0, 1 - h].astype(F32) + a2[1, 1 - h].astype(F32)
    ).astype(BF16)
    a_flip = remote(p_a.at[z, 1 - h], a3, flip)

    b_up.wait_recv()
    add(p_b.at[zz(1), h, 0:96], b2.at[0])
    b_up2 = remote(p_b.at[zz(1), h], b3.at[0], up)
    b_down.wait_recv()
    add(p_b.at[zz(3), h, 96:192], b2.at[1])
    b_down2 = remote(p_b.at[zz(3), h], b3.at[1], down)

    for copy in m_copies:
        copy.wait_recv()
    total = m_part[here].astype(F32)
    for index in range(7):
        total = total + m_recv[index].astype(F32)
    m_own[...] = total.astype(BF16)
    ga[slot(0, 0), :, TA:] = m_own[...]
    x_proj = tn(proj_ref[...], xall[col])

    conv_copy.wait()
    head = head_ref[...]
    taps = [jnp.sum(conv[k].astype(F32) * head, axis=1, keepdims=True) for k in range(9)]
    lane = lax.broadcasted_iota(jnp.int32, (16, CH), 1)
    sub = lax.broadcasted_iota(jnp.int32, (16, CH), 0)
    head_col = jnp.sum(jnp.where(lane == sub + first_channel, head, 0.0), axis=1, keepdims=True)

    b_copies[0].wait_recv()
    a_flip.wait_recv()
    pre[:, :TA] = (
        p_a[z, h].astype(F32) + a2[0, h].astype(F32) + a2[1, h].astype(F32) + a3[...].astype(F32)
    )
    b_up2.wait_recv()
    b_down2.wait_recv()
    pre[:, TA:] = (
        p_b[z, h].astype(F32) + b1[z].astype(F32) + b3[0].astype(F32) + b3[1].astype(F32)
    )

    @pl.loop(0, TOK // 128)
    def _(t):
        at = pl.ds(pl.multiple_of(t * 128, 128), 128)
        value = pre[:, at]
        hid[:, at] = (value * cdf(value)).astype(BF16)

    @pl.loop(0, TOK // 256)
    def _(t):
        at = pl.ds(pl.multiple_of(t * 256, 256), 256)
        zc[:, at] = tn(m_own[...], hid[:, at])

    strip = pl.ds(pl.multiple_of(col * STRIP, STRIP), STRIP)
    zc[:, strip] = zc[:, strip] + x_proj

    z1[...] = zc[pl.ds(pl.multiple_of(other * 128, 128), 128), :].astype(BF16)
    z1_copy = remote(z1, z1_recv, partner)

    bulk_from = len(sent)
    mine_a, mine_b = ga.at[slot(0, 0)], gb.at[slot(0, 0)]
    pair = []

    def send(buf, dz, dh, device, rows=None):
        ref = buf.at[slot(dz, dh)] if rows is None else buf.at[slot(dz, dh), rows[0] : rows[1]]
        return remote(ref, ref, device)

    top, low = (0, 96), (96, 192)

    @pl.loop(0, TB // 128)
    def _(t):
        at = pl.ds(pl.multiple_of(t * 128, 128), 128)
        mine_b[:, at] = slope(pre[:, pl.ds(pl.multiple_of(TA + t * 128, 128), 128)]).astype(BF16)

    bu = send(gb, 0, 0, up)
    bd = send(gb, 0, 0, down)
    pair.append(send(gb, 0, 0, partner))

    @pl.loop(0, TA // 128)
    def _(t):
        at = pl.ds(pl.multiple_of(t * 128, 128), 128)
        mine_a[:, at] = slope(pre[:, at]).astype(BF16)

    fa = send(ga, 0, 0, flip)
    pair.append(send(ga, 0, 0, partner))

    z1_copy.wait_recv()
    z2[...] = (
        zc[pl.ds(pl.multiple_of(c * 128, 128), 128), :] + z1_recv[...].astype(F32)
    ).astype(BF16)
    z2_copies = []
    for index, (dz, dh) in enumerate(chip_peers):
        at = pl.multiple_of((zz(dz) * 2 + hh(dh)) * 16, 16)
        z2_copies.append(remote(z2.at[pl.ds(at, 16)], z2_recv.at[index], at_row(dz, dh, 0)))
    fb = send(gb, 0, 0, flip)
    au = send(ga, 0, 0, up)
    ad = send(ga, 0, 0, down)
    bu.wait_recv()
    bu2 = send(gb, 3, 0, up, top)
    f_m = send(gb, 3, 0, flip)
    pair.append(send(gb, 3, 0, partner))
    bd.wait_recv()
    bd2 = send(gb, 1, 0, down, low)
    f_p = send(gb, 1, 0, flip)
    pair.append(send(gb, 1, 0, partner))
    part = z2[pl.ds(pl.multiple_of(here * 16, 16), 16), :].astype(F32)
    for index, copy in enumerate(z2_copies):
        copy.wait_recv()
        part = part + z2_recv[index].astype(F32)
    z3[col] = part.astype(BF16)
    z3_copies = [remote(z3.at[col], z3.at[col], at_col(*peer)) for peer in col_peers]
    fa.wait_recv()
    fau = send(ga, 0, 1, up)
    fad = send(ga, 0, 1, down)
    pair.append(send(ga, 0, 1, partner))
    for copy in z3_copies:
        copy.wait_recv()
    field = z3[0].astype(F32)
    for index in range(1, 8):
        field = field + z3[index].astype(F32)

    token = lax.broadcasted_iota(jnp.int32, (1, TOK), 1)
    line, place = token >> 6, token & (GW - 1)

    def moved(values, di, dj):
        shift = di * GW + dj
        if shift:
            values = pltpu.roll(values, (-shift) % TOK, 1)
        inside = (
            (line + di >= 0) & (line + di < GH) & (place + dj >= 0) & (place + dj < GW)
        )
        return jnp.where(inside, values, 0.0)

    act = (field * cdf(field)).astype(BF16).astype(F32)
    pred = jnp.sum(field * head_col, axis=0, keepdims=True)
    for k in range(9):
        pred = pred + moved(jnp.sum(act * taps[k], axis=0, keepdims=True), k // 3 - 1, k % 3 - 1)
    for index in range(8):
        rows_buf[index : index + 1, :] = pred[:, index * STRIP : (index + 1) * STRIP]
    pred_all[row] = rows_buf[...]
    pred_copies = [remote(pred_all.at[row], pred_all.at[row], at_row(*peer)) for peer in row_peers]
    fb.wait_recv()
    pair.append(send(gb, 0, 1, partner))
    bu2.wait_recv()
    f_top = send(gb, 2, 0, flip, top)
    pair.append(send(gb, 2, 0, partner, top))
    bd2.wait_recv()
    f_low = send(gb, 2, 0, flip, low)
    pair.append(send(gb, 2, 0, partner, low))
    au.wait_recv()
    au2 = send(ga, 3, 0, up)
    pair.append(send(ga, 3, 0, partner))
    ad.wait_recv()
    pair.append(send(ga, 1, 0, partner))
    field_slope = slope(field)
    valid = jnp.concatenate([st_col[index][2:3] for index in range(8)], axis=0)
    target = jnp.concatenate([st_col[index][3:4] for index in range(8)], axis=0)
    for copy in pred_copies:
        copy.wait_recv()
    pred = pred_all[0]
    for index in range(1, 16):
        pred = pred + pred_all[index]

    err = valid * (pred - target)

    def whole(values):
        return jnp.sum(jnp.sum(values, axis=1, keepdims=True), axis=0, keepdims=True)

    count = whole(valid)
    mean_err = whole(err) / count
    loss_ref[0, 0] = jnp.sum(whole(err * err) / count - FOCUS * mean_err * mean_err)
    grad_pred = valid * (2.0 * err - 2.0 * FOCUS * mean_err)
    grad_pred = jnp.concatenate([grad_pred[index : index + 1] for index in range(8)], axis=1)
    back = jnp.zeros((16, TOK), F32)
    for k in range(9):
        back = back + taps[k] * moved(grad_pred, 1 - k // 3, 1 - k % 3)
    mine = pl.ds(first_channel, 16)
    gz[mine, :] = (grad_pred * head_col + field_slope * back).astype(BF16)

    gz_copies = [
        remote(gz.at[mine], gz.at[mine], at_row(dz, dh, 0)) for dz, dh in chip_peers
    ]
    gz_pair = [remote(gz.at[mine], gz.at[mine], partner)]
    f_m.wait_recv()
    pair.append(send(gb, 3, 1, partner))
    fad.wait_recv()
    fad2 = send(ga, 1, 1, down)
    pair.append(send(ga, 1, 1, partner))
    fau.wait_recv()
    pair.append(send(ga, 3, 1, partner))
    f_p.wait_recv()
    pair.append(send(gb, 1, 1, partner))
    for (dz, dh), copy in zip(chip_peers, gz_copies):
        copy.wait_recv()
        came = gz.at[pl.ds(pl.multiple_of(c * 128 + (zz(-dz) * 2 + hh(dh)) * 16, 16), 16)]
        gz_pair.append(remote(came, came, partner))
    for copy in gz_pair:
        copy.wait_recv()

    gh_own[...] = nt(hid[...], gz[...]).astype(BF16)
    local(gh_own, gh_out.at[slot(0, 0)])
    bulk_to = len(sent)
    gh_copies = [
        remote(gh_own, gh_out.at[slot(0, 0)], at_row(dz, dh, 0)) for dz, dh in chip_peers
    ]
    gh_pair = [remote(gh_own, gh_out.at[slot(0, 0)], partner)]
    bulk_end = len(sent)
    f_top.wait_recv()
    pair.append(send(gb, 2, 1, partner, top))
    f_low.wait_recv()
    pair.append(send(gb, 2, 1, partner, low))
    au2.wait_recv()
    pair.append(send(ga, 2, 0, partner))
    fad2.wait_recv()
    pair.append(send(ga, 2, 1, partner))
    for copy in pair:
        copy.wait_recv()
    bulk = sent[bulk_from:bulk_to] + sent[bulk_end:]
    for copy in bulk:
        copy.wait_send()

    @pl.loop(0, 16)
    def _(k):
        weights = ga[k, :, TA:]
        ga[k, :, :TA] = (mm(weights, gz[:, :TA]) * ga[k, :, :TA].astype(F32)).astype(BF16)
        gb[k] = (mm(weights, gz[:, TA:]) * gb[k].astype(F32)).astype(BF16)
        pltpu.make_async_copy(ga.at[k, :, :TA], gp_out.at[k, :, :TA], out_sems.at[0, k]).start()
        pltpu.make_async_copy(gb.at[k], gp_out.at[k, :, TA:], out_sems.at[1, k]).start()

    for (dz, dh), copy in zip(chip_peers, gh_copies):
        copy.wait_recv()
        came = gh_out.at[slot(-dz, dh)]
        gh_pair.append(remote(came, came, partner))
    for copy in gh_pair:
        copy.wait_recv()

    @pl.loop(0, 16)
    def _(k):
        pltpu.make_async_copy(ga.at[k, :, :TA], gp_out.at[k, :, :TA], out_sems.at[0, k]).wait()
        pltpu.make_async_copy(gb.at[k], gp_out.at[k, :, TA:], out_sems.at[1, k]).wait()

    for copy in started[-2:]:
        copy.wait()
    for copy in sent:
        if not any(copy is other_copy for other_copy in bulk):
            copy.wait_send()


def weight_kernel(n_ref, gp_ref, gh_ref, proj_ref, up_ref, down_ref):
    up_ref[...] = nt(n_ref[...], gp_ref[...].reshape(2 * OWN, TOK))
    down_ref[...] = nt(gh_ref[...].reshape(2 * OWN, CH), proj_ref[...])


def on_device(tokens, ln_gain, w_up, w_down, proj, conv_kernel, head_weight, depth_mm, lidar_mask):
    vmem = pl.BlockSpec(memory_space=pltpu.VMEM)
    anywhere = pl.BlockSpec(memory_space=pl.ANY)
    normed, grad_pre, grad_hidden, loss = pl.pallas_call(
        step_kernel,
        name="mlp_step",
        out_shape=[
            jax.ShapeDtypeStruct((FEAT, TOK), BF16),
            jax.ShapeDtypeStruct((16, OWN, TOK), BF16),
            jax.ShapeDtypeStruct((16, OWN, CH), BF16),
            jax.ShapeDtypeStruct((1, 1), F32),
        ],
        in_specs=[
            anywhere, vmem, anywhere, anywhere, anywhere, anywhere, vmem, anywhere, anywhere,
        ],
        out_specs=[anywhere, anywhere, anywhere, pl.BlockSpec(memory_space=pltpu.SMEM)],
        scratch_shapes=[
            pltpu.VMEM((STRIP, FEAT), BF16),
            pltpu.VMEM((FEAT, HID), BF16),
            pltpu.VMEM((HID, FEAT), BF16),
            pltpu.VMEM((FEAT, CH), BF16),
            pltpu.VMEM((9, 16, CH), BF16),
            pltpu.VMEM((2, GW), jnp.int32),
            pltpu.VMEM((2, GW), jnp.int32),
            pltpu.VMEM((8, FEAT, STRIP), BF16),
            pltpu.VMEM((16, 8, STRIP), F32),
            pltpu.VMEM((8, 8, STRIP), F32),
            pltpu.VMEM((HALF, 2 * FEAT), BF16),
            pltpu.VMEM((HALF, FEAT), BF16),
            pltpu.VMEM((HALF, FEAT), BF16),
            pltpu.VMEM((FEAT, CH), BF16),
            pltpu.VMEM((2 * FEAT, TOK), BF16),
            pltpu.VMEM((8, OWN, CH), F32),
            pltpu.VMEM((8, OWN, CH), BF16),
            pltpu.VMEM((7, OWN, CH), BF16),
            pltpu.VMEM((OWN, CH), BF16),
            pltpu.VMEM((4, 2, OWN, TA), BF16),
            pltpu.VMEM((4, 2, OWN, TB), BF16),
            pltpu.VMEM((2, OWN, TA), BF16),
            pltpu.VMEM((2, 2, OWN, TA), BF16),
            pltpu.VMEM((OWN, TA), BF16),
            pltpu.VMEM((4, OWN, TB), BF16),
            pltpu.VMEM((2, OWN // 2, TB), BF16),
            pltpu.VMEM((2, OWN, TB), BF16),
            pltpu.VMEM((OWN, TOK), F32),
            pltpu.VMEM((OWN, TOK), BF16),
            pltpu.VMEM((CH, TOK), F32),
            pltpu.VMEM((128, TOK), BF16),
            pltpu.VMEM((128, TOK), BF16),
            pltpu.VMEM((128, TOK), BF16),
            pltpu.VMEM((7, 16, TOK), BF16),
            pltpu.VMEM((8, 16, TOK), BF16),
            pltpu.VMEM((16, 8, STRIP), F32),
            pltpu.VMEM((8, STRIP), F32),
            pltpu.VMEM((CH, TOK), BF16),
            pltpu.VMEM((16, OWN, GA), BF16),
            pltpu.VMEM((16, OWN, TB), BF16),
            pltpu.VMEM((OWN, CH), BF16),
            pltpu.SemaphoreType.DMA((N_SEMS,)),
            pltpu.SemaphoreType.DMA((N_SEMS,)),
            pltpu.SemaphoreType.DMA((9,)),
            pltpu.SemaphoreType.DMA((2, 16)),
        ],
        compiler_params=pltpu.CompilerParams(
            collective_id=0, has_side_effects=True, vmem_limit_bytes=60 * 2**20
        ),
        cost_estimate=pl.CostEstimate(flops=6 * 10**9, bytes_accessed=16 * 2**20, transcendentals=10**6),
    )(
        tokens, ln_gain, w_up, w_down, proj, conv_kernel.reshape(9, CH, CH),
        head_weight.reshape(1, CH), depth_mm, lidar_mask,
    )
    grad_up, grad_down = pl.pallas_call(
        weight_kernel,
        name="weight_grads",
        grid=(8,),
        out_shape=[
            jax.ShapeDtypeStruct((FEAT, HID), F32),
            jax.ShapeDtypeStruct((HID, FEAT), F32),
        ],
        in_specs=[
            pl.BlockSpec((FEAT, TOK), lambda j: (0, 0)),
            pl.BlockSpec((2, OWN, TOK), lambda j: (j, 0, 0)),
            pl.BlockSpec((2, OWN, CH), lambda j: (j, 0, 0)),
            pl.BlockSpec((FEAT, CH), lambda j: (0, 0)),
        ],
        out_specs=[
            pl.BlockSpec((FEAT, 2 * OWN), lambda j: (0, j)),
            pl.BlockSpec((2 * OWN, FEAT), lambda j: (j, 0)),
        ],
        compiler_params=pltpu.CompilerParams(vmem_limit_bytes=60 * 2**20),
        cost_estimate=pl.CostEstimate(flops=3 * 10**9, bytes_accessed=18 * 2**20, transcendentals=0),
    )(normed, grad_pre, grad_hidden, proj)
    return (grad_up, grad_down, loss.reshape(()))


def solution(mesh):
    return jax.shard_map(
        on_device,
        mesh=mesh,
        in_specs=(
            P("col", "row"),
            P("row"),
            P("row", "col"),
            P("col", "row"),
            P("row", None),
            P(),
            P(),
            P("col", None),
            P("col", None),
        ),
        out_specs=(P("row", "col"), P("col", "row"), P()),
        check_vma=False,
    )
```

time: 137 us -> 129 us (0.942)
  the two profiles are of different devices: /device:TPU:1 before, /device:TPU:59 now
where the time goes in v2:
time: 129 us
  Pallas kernels  126 us (98%)
  between operations  2.39 us (2%)
    pallas_call x1, Pallas kernels, on_device(): pl.pallas_call(step_kernel, name='mlp_step', out_shape=[jax.ShapeDtypeStr...  116 us
    pallas_call x1, Pallas kernels, on_device(): pl.pallas_call(weight_kernel, name='weight_grads', grid=(8,), out_shape=[...  10.6 us

profile of v2, /device:TPU:59, one launch (start us, length us, event | category | flops | bytes accessed | tf_op | source)
XLA Modules:
  0.0 128.8 jit_solution(16381046142928132568)
XLA Ops:
  0.6 115.8 %mlp_step.1 = (bf16[384,1024]{1,0:T(8,128)(2,1)}, bf16[16,192,1024]{2,1,0:T(8,128)(2,1)}, bf16[16,192,256]{2,1,0:T(8,128)(2,1)}, f32[1,1]{1,0:T(1,128)}) custom-call(bf16[128,384]{1,0:T(8,128)(2,1)} %tok_hbm.1, f32[384]{0:T(512)} %gain_ref.1, bf16[384,3072]{1,0:T(8,128)(2,1)} %wup_hbm.1, bf16[3072,384]{1,0:T(8,128)(2,1)} %wdn_hbm.1, ...), custom_call_target="tpu_custom_call" | custom-call | flops 6000000000 | bytes 16777216 | tf_op jit(solution)/shard_map/mlp_step/pallas_call | solution.py:524
  116.4 10.6 %weight_grads.1 = (f32[384,3072]{1,0:T(8,128)}, f32[3072,384]{1,0:T(8,128)}) custom-call(bf16[384,1024]{1,0:T(8,128)(2,1)} %get-tuple-element.9.n_ref, bf16[16,192,1024]{2,1,0:T(8,128)(2,1)} %get-tuple-element.10.gp_ref, bf16[16,192,256]{2,1,0:T(8,128)(2,1)} %get-tuple-element.11.gh_ref, bf16[384,256]{1,0:T(8,128)(2,1)} %proj_ref.1), custom_call_target="tpu_custom_call" | custom-call | flops 3000000000 | bytes 18874368 | tf_op jit(solution)/shard_map/weight_grads/pallas_call | solution.py:592

commit v3 on v2

--- a/solution.py
+++ b/solution.py
@@ -59,7 +59,7 @@
     tok_ref, wup_ref, wdn, proj_ref, conv, depth_ref, mask_ref,
     xall, st_row, st_col, w_t, w_send, wd_peer, proj_peer, n_t, m_sum, m_part, m_recv, m_own,
     p_a, p_b, a1, a2, a3, b1, b2, b3, pre, hid, zc, z1, z1_recv, z2, z2_recv, z3,
-    pred_all, rows_buf, gz, ga, gb, gh_own, send_sems, recv_sems, local_sems, out_sems,
+    taps, field, field_slope, shifted, pred_all, rows_buf, gz, ga, gb, gh_own, send_sems, recv_sems, local_sems, out_sems,
 ):
     row, col = lax.axis_index("row"), lax.axis_index("col")
     z, h, c = row // 4, lax.rem(row // 2, 2), lax.rem(row, 2)
@@ -91,6 +91,9 @@
     def slot(dz, dh):
         return c * 8 + zz(dz) * 2 + hh(dh)
 
+    def own_rows(dz, dh):
+        return pl.ds(pl.multiple_of(slot(dz, dh) * OWN, 64), OWN)
+
     sent = []
     row_peers = [
         (dz, dh, dc) for dz in (2, 1, 3, 0) for dh in (1, 0) for dc in (1, 0) if (dz, dh, dc) != (0, 0, 0)
@@ -115,14 +118,14 @@
         started.append(copy)
         return copy
 
-    first_channel = pl.multiple_of(c * 128 + here * 16, 16)
+    first_channel = pl.multiple_of(c * 128, 128)
     tok_copy = local(tok_hbm, tok_ref)
     proj_in = local(proj_hbm, proj_ref)
     wdn_copy = local(wdn_hbm, wdn)
     wup_copy = local(wup_hbm, wup_ref)
     depth_copy = local(depth_hbm, depth_ref)
     mask_copy = local(mask_hbm, mask_ref)
-    conv_copy = local(conv_hbm.at[:, pl.ds(first_channel, 16), :], conv)
+    conv_copy = local(conv_hbm.at[:, pl.ds(first_channel, 128), :], conv)
 
     tok_copy.wait()
     x_t = tok_ref[...].astype(F32).T
@@ -147,7 +150,8 @@
     pl.semaphore_wait(barrier, len(row_peers) + len(col_peers))
 
     stat_copies = [remote(st_row.at[row], st_row.at[row], at_row(*peer)) for peer in row_peers]
-    token_copies = [remote(xall.at[col], xall.at[col], at_col(*peer)) for peer in col_peers]
+    across = remote(xall.at[col], xall.at[col], at_col(1, 0))
+    token_copies = [remote(xall.at[col], xall.at[col], at_col(0, dx)) for dx in (2, 1, 3)]
     wd_copy = remote(wdn.at[pl.ds(to_peer, HALF)], wd_peer, partner)
     proj_copy = remote(proj_ref, proj_peer, partner)
 
@@ -159,6 +163,9 @@
         at = pl.multiple_of(to_peer + i * 128, 128)
         w_send[pl.ds(pl.multiple_of(i * 128, 128), 128), :] = wup_ref[:, pl.ds(at, 128)].T
 
+    across.wait_recv()
+    came = xall.at[lax.rem(col + 4, 8)]
+    token_copies += [remote(came, came, at_col(0, dx)) for dx in (2, 1, 3)]
     w_copy = remote(w_send, w_t.at[:, pl.ds(feature_at, FEAT)], partner)
 
     for copy in stat_copies:
@@ -291,10 +298,15 @@
 
     conv_copy.wait()
     head = head_ref[...]
-    taps = [jnp.sum(conv[k].astype(F32) * head, axis=1, keepdims=True) for k in range(9)]
-    lane = lax.broadcasted_iota(jnp.int32, (16, CH), 1)
-    sub = lax.broadcasted_iota(jnp.int32, (16, CH), 0)
-    head_col = jnp.sum(jnp.where(lane == sub + first_channel, head, 0.0), axis=1, keepdims=True)
+    for k in range(9):
+        taps[k] = jnp.broadcast_to(
+            jnp.sum(conv[k].astype(F32) * head, axis=1, keepdims=True), (128, 128)
+        )
+    lane = lax.broadcasted_iota(jnp.int32, (128, CH), 1)
+    sub = lax.broadcasted_iota(jnp.int32, (128, CH), 0)
+    taps[9] = jnp.broadcast_to(
+        jnp.sum(jnp.where(lane == sub + first_channel, head, 0.0), axis=1, keepdims=True), (128, 128)
+    )
 
     b_copies[0].wait_recv()
     a_flip.wait_recv()
@@ -339,17 +351,10 @@
         at = pl.ds(pl.multiple_of(t * 128, 128), 128)
         mine_b[:, at] = slope(pre[:, pl.ds(pl.multiple_of(TA + t * 128, 128), 128)]).astype(BF16)
 
-    bu = send(gb, 0, 0, up)
-    bd = send(gb, 0, 0, down)
-    pair.append(send(gb, 0, 0, partner))
-
     @pl.loop(0, TA // 128)
     def _(t):
         at = pl.ds(pl.multiple_of(t * 128, 128), 128)
         mine_a[:, at] = slope(pre[:, at]).astype(BF16)
-
-    fa = send(ga, 0, 0, flip)
-    pair.append(send(ga, 0, 0, partner))
 
     z1_copy.wait_recv()
     z2[...] = (
@@ -359,32 +364,46 @@
     for index, (dz, dh) in enumerate(chip_peers):
         at = pl.multiple_of((zz(dz) * 2 + hh(dh)) * 16, 16)
         z2_copies.append(remote(z2.at[pl.ds(at, 16)], z2_recv.at[index], at_row(dz, dh, 0)))
-    fb = send(gb, 0, 0, flip)
+    bu = send(gb, 0, 0, up)
+    bd = send(gb, 0, 0, down)
+    fa = send(ga, 0, 0, flip)
+    pair.append(send(gb, 0, 0, partner))
+    pair.append(send(ga, 0, 0, partner))
+    mine = pl.ds(pl.multiple_of(here * 16, 16), 16)
+    part = z2[mine, :].astype(F32)
+    for index, copy in enumerate(z2_copies):
+        copy.wait_recv()
+        part = part + z2_recv[index].astype(F32)
+    z3[col] = part.astype(BF16)
+    z3_copies = [remote(z3.at[col], z3.at[col], at_col(*peer)) for peer in col_peers]
     au = send(ga, 0, 0, up)
     ad = send(ga, 0, 0, down)
+    fb = send(gb, 0, 0, flip)
     bu.wait_recv()
     bu2 = send(gb, 3, 0, up, top)
-    f_m = send(gb, 3, 0, flip)
     pair.append(send(gb, 3, 0, partner))
     bd.wait_recv()
     bd2 = send(gb, 1, 0, down, low)
+    pair.append(send(gb, 1, 0, partner))
+    for copy in z3_copies:
+        copy.wait_recv()
+    total = z3[0].astype(F32)
+    for index in range(1, 8):
+        total = total + z3[index].astype(F32)
+    field[mine, :] = total.astype(BF16)
+    z4_copies = [
+        remote(field.at[mine], field.at[mine], at_row(dz, dh, 0)) for dz, dh in chip_peers
+    ]
+    f_m = send(gb, 3, 0, flip)
     f_p = send(gb, 1, 0, flip)
-    pair.append(send(gb, 1, 0, partner))
-    part = z2[pl.ds(pl.multiple_of(here * 16, 16), 16), :].astype(F32)
-    for index, copy in enumerate(z2_copies):
-        copy.wait_recv()
-        part = part + z2_recv[index].astype(F32)
-    z3[col] = part.astype(BF16)
-    z3_copies = [remote(z3.at[col], z3.at[col], at_col(*peer)) for peer in col_peers]
     fa.wait_recv()
     fau = send(ga, 0, 1, up)
     fad = send(ga, 0, 1, down)
     pair.append(send(ga, 0, 1, partner))
-    for copy in z3_copies:
-        copy.wait_recv()
-    field = z3[0].astype(F32)
-    for index in range(1, 8):
-        field = field + z3[index].astype(F32)
+    fb.wait_recv()
+    pair.append(send(gb, 0, 1, partner))
+    for copy in z4_copies:
+        copy.wait_recv()
 
     token = lax.broadcasted_iota(jnp.int32, (1, TOK), 1)
     line, place = token >> 6, token & (GW - 1)
@@ -398,16 +417,22 @@
         )
         return jnp.where(inside, values, 0.0)
 
-    act = (field * cdf(field)).astype(BF16).astype(F32)
-    pred = jnp.sum(field * head_col, axis=0, keepdims=True)
+    @pl.loop(0, TOK // 128)
+    def _(t):
+        at = pl.ds(pl.multiple_of(t * 128, 128), 128)
+        value = field[:, at].astype(F32)
+        act = (value * cdf(value)).astype(BF16).astype(F32)
+        for k in range(9):
+            shifted[k : k + 1, at] = jnp.sum(act * taps[k], axis=0, keepdims=True)
+        shifted[9:10, at] = jnp.sum(value * taps[9], axis=0, keepdims=True)
+
+    pred = shifted[9:10, :]
     for k in range(9):
-        pred = pred + moved(jnp.sum(act * taps[k], axis=0, keepdims=True), k // 3 - 1, k % 3 - 1)
+        pred = pred + moved(shifted[k : k + 1, :], k // 3 - 1, k % 3 - 1)
     for index in range(8):
         rows_buf[index : index + 1, :] = pred[:, index * STRIP : (index + 1) * STRIP]
-    pred_all[row] = rows_buf[...]
-    pred_copies = [remote(pred_all.at[row], pred_all.at[row], at_row(*peer)) for peer in row_peers]
-    fb.wait_recv()
-    pair.append(send(gb, 0, 1, partner))
+    pred_all[c] = rows_buf[...]
+    pred_copy = remote(pred_all.at[c], pred_all.at[c], partner)
     bu2.wait_recv()
     f_top = send(gb, 2, 0, flip, top)
     pair.append(send(gb, 2, 0, partner, top))
@@ -419,16 +444,16 @@
     pair.append(send(ga, 3, 0, partner))
     ad.wait_recv()
     pair.append(send(ga, 1, 0, partner))
-    field_slope = slope(field)
+
+    @pl.loop(0, TOK // 128)
+    def _(t):
+        at = pl.ds(pl.multiple_of(t * 128, 128), 128)
+        field_slope[:, at] = slope(field[:, at].astype(F32))
+
     valid = jnp.concatenate([st_col[index][2:3] for index in range(8)], axis=0)
     target = jnp.concatenate([st_col[index][3:4] for index in range(8)], axis=0)
-    for copy in pred_copies:
-        copy.wait_recv()
-    pred = pred_all[0]
-    for index in range(1, 16):
-        pred = pred + pred_all[index]
-
-    err = valid * (pred - target)
+    pred_copy.wait_recv()
+    err = valid * (pred_all[0] + pred_all[1] - target)
 
     def whole(values):
         return jnp.sum(jnp.sum(values, axis=1, keepdims=True), axis=0, keepdims=True)
@@ -438,16 +463,36 @@
     loss_ref[0, 0] = jnp.sum(whole(err * err) / count - FOCUS * mean_err * mean_err)
     grad_pred = valid * (2.0 * err - 2.0 * FOCUS * mean_err)
     grad_pred = jnp.concatenate([grad_pred[index : index + 1] for index in range(8)], axis=1)
-    back = jnp.zeros((16, TOK), F32)
     for k in range(9):
-        back = back + taps[k] * moved(grad_pred, 1 - k // 3, 1 - k % 3)
-    mine = pl.ds(first_channel, 16)
-    gz[mine, :] = (grad_pred * head_col + field_slope * back).astype(BF16)
-
-    gz_copies = [
-        remote(gz.at[mine], gz.at[mine], at_row(dz, dh, 0)) for dz, dh in chip_peers
+        shifted[k : k + 1, :] = moved(grad_pred, 1 - k // 3, 1 - k % 3)
+    shifted[9:10, :] = grad_pred
+
+    @pl.loop(0, TOK // 128)
+    def _(t):
+        at = pl.ds(pl.multiple_of(t * 128, 128), 128)
+        back = taps[0] * shifted[0:1, at]
+        for k in range(1, 9):
+            back = back + taps[k] * shifted[k : k + 1, at]
+        gz[pl.ds(first_channel, 128), at] = (
+            taps[9] * shifted[9:10, at] + field_slope[:, at] * back
+        ).astype(BF16)
+
+    half_z = gz.at[pl.ds(first_channel, 128)]
+    gz_copy = remote(half_z, half_z, partner)
+
+    second_channel = pl.multiple_of(other * 128, 128)
+    gh_own[:, pl.ds(first_channel, 128)] = nt(hid[...], half_z[...]).astype(BF16)
+    gz_copy.wait_recv()
+    gh_own[:, pl.ds(second_channel, 128)] = nt(
+        hid[...], gz[pl.ds(second_channel, 128), :]
+    ).astype(BF16)
+    local(gh_own, gh_out.at[own_rows(0, 0)])
+    bulk_to = len(sent)
+    gh_copies = [
+        remote(gh_own, gh_out.at[own_rows(0, 0)], at_row(dz, dh, 0)) for dz, dh in chip_peers
     ]
-    gz_pair = [remote(gz.at[mine], gz.at[mine], partner)]
+    gh_pair = [remote(gh_own, gh_out.at[own_rows(0, 0)], partner)]
+    bulk_end = len(sent)
     f_m.wait_recv()
     pair.append(send(gb, 3, 1, partner))
     fad.wait_recv()
@@ -457,21 +502,6 @@
     pair.append(send(ga, 3, 1, partner))
     f_p.wait_recv()
     pair.append(send(gb, 1, 1, partner))
-    for (dz, dh), copy in zip(chip_peers, gz_copies):
-        copy.wait_recv()
-        came = gz.at[pl.ds(pl.multiple_of(c * 128 + (zz(-dz) * 2 + hh(dh)) * 16, 16), 16)]
-        gz_pair.append(remote(came, came, partner))
-    for copy in gz_pair:
-        copy.wait_recv()
-
-    gh_own[...] = nt(hid[...], gz[...]).astype(BF16)
-    local(gh_own, gh_out.at[slot(0, 0)])
-    bulk_to = len(sent)
-    gh_copies = [
-        remote(gh_own, gh_out.at[slot(0, 0)], at_row(dz, dh, 0)) for dz, dh in chip_peers
-    ]
-    gh_pair = [remote(gh_own, gh_out.at[slot(0, 0)], partner)]
-    bulk_end = len(sent)
     f_top.wait_recv()
     pair.append(send(gb, 2, 1, partner, top))
     f_low.wait_recv()
@@ -491,20 +521,20 @@
         weights = ga[k, :, TA:]
         ga[k, :, :TA] = (mm(weights, gz[:, :TA]) * ga[k, :, :TA].astype(F32)).astype(BF16)
         gb[k] = (mm(weights, gz[:, TA:]) * gb[k].astype(F32)).astype(BF16)
-        pltpu.make_async_copy(ga.at[k, :, :TA], gp_out.at[k, :, :TA], out_sems.at[0, k]).start()
-        pltpu.make_async_copy(gb.at[k], gp_out.at[k, :, TA:], out_sems.at[1, k]).start()
+        pltpu.make_async_copy(ga.at[k, :, :TA], gp_out.at[pl.ds(pl.multiple_of(k * OWN, 64), OWN), :TA], out_sems.at[0, k]).start()
+        pltpu.make_async_copy(gb.at[k], gp_out.at[pl.ds(pl.multiple_of(k * OWN, 64), OWN), TA:], out_sems.at[1, k]).start()
 
     for (dz, dh), copy in zip(chip_peers, gh_copies):
         copy.wait_recv()
-        came = gh_out.at[slot(-dz, dh)]
+        came = gh_out.at[own_rows(-dz, dh)]
         gh_pair.append(remote(came, came, partner))
     for copy in gh_pair:
         copy.wait_recv()
 
     @pl.loop(0, 16)
     def _(k):
-        pltpu.make_async_copy(ga.at[k, :, :TA], gp_out.at[k, :, :TA], out_sems.at[0, k]).wait()
-        pltpu.make_async_copy(gb.at[k], gp_out.at[k, :, TA:], out_sems.at[1, k]).wait()
+        pltpu.make_async_copy(ga.at[k, :, :TA], gp_out.at[pl.ds(pl.multiple_of(k * OWN, 64), OWN), :TA], out_sems.at[0, k]).wait()
+        pltpu.make_async_copy(gb.at[k], gp_out.at[pl.ds(pl.multiple_of(k * OWN, 64), OWN), TA:], out_sems.at[1, k]).wait()
 
     for copy in started[-2:]:
         copy.wait()
@@ -514,8 +544,8 @@
 
 
 def weight_kernel(n_ref, gp_ref, gh_ref, proj_ref, up_ref, down_ref):
-    up_ref[...] = nt(n_ref[...], gp_ref[...].reshape(2 * OWN, TOK))
-    down_ref[...] = nt(gh_ref[...].reshape(2 * OWN, CH), proj_ref[...])
+    up_ref[...] = nt(n_ref[...], gp_ref[...])
+    down_ref[...] = nt(gh_ref[...], proj_ref[...])
 
 
 def on_device(tokens, ln_gain, w_up, w_down, proj, conv_kernel, head_weight, depth_mm, lidar_mask):
@@ -526,8 +556,8 @@
         name="mlp_step",
         out_shape=[
             jax.ShapeDtypeStruct((FEAT, TOK), BF16),
-            jax.ShapeDtypeStruct((16, OWN, TOK), BF16),
-            jax.ShapeDtypeStruct((16, OWN, CH), BF16),
+            jax.ShapeDtypeStruct((HID, TOK), BF16),
+            jax.ShapeDtypeStruct((HID, CH), BF16),
             jax.ShapeDtypeStruct((1, 1), F32),
         ],
         in_specs=[
@@ -539,7 +569,7 @@
             pltpu.VMEM((FEAT, HID), BF16),
             pltpu.VMEM((HID, FEAT), BF16),
             pltpu.VMEM((FEAT, CH), BF16),
-            pltpu.VMEM((9, 16, CH), BF16),
+            pltpu.VMEM((9, 128, CH), BF16),
             pltpu.VMEM((2, GW), jnp.int32),
             pltpu.VMEM((2, GW), jnp.int32),
             pltpu.VMEM((8, FEAT, STRIP), BF16),
@@ -570,7 +600,11 @@
             pltpu.VMEM((128, TOK), BF16),
             pltpu.VMEM((7, 16, TOK), BF16),
             pltpu.VMEM((8, 16, TOK), BF16),
-            pltpu.VMEM((16, 8, STRIP), F32),
+            pltpu.VMEM((10, 128, 128), F32),
+            pltpu.VMEM((128, TOK), BF16),
+            pltpu.VMEM((128, TOK), F32),
+            pltpu.VMEM((16, TOK), F32),
+            pltpu.VMEM((2, 8, STRIP), F32),
             pltpu.VMEM((8, STRIP), F32),
             pltpu.VMEM((CH, TOK), BF16),
             pltpu.VMEM((16, OWN, GA), BF16),
@@ -592,20 +626,20 @@
     grad_up, grad_down = pl.pallas_call(
         weight_kernel,
         name="weight_grads",
-        grid=(8,),
+        grid=(HID // 512,),
         out_shape=[
             jax.ShapeDtypeStruct((FEAT, HID), F32),
             jax.ShapeDtypeStruct((HID, FEAT), F32),
         ],
         in_specs=[
             pl.BlockSpec((FEAT, TOK), lambda j: (0, 0)),
-            pl.BlockSpec((2, OWN, TOK), lambda j: (j, 0, 0)),
-            pl.BlockSpec((2, OWN, CH), lambda j: (j, 0, 0)),
+            pl.BlockSpec((512, TOK), lambda j: (j, 0)),
+            pl.BlockSpec((512, CH), lambda j: (j, 0)),
             pl.BlockSpec((FEAT, CH), lambda j: (0, 0)),
         ],
         out_specs=[
-            pl.BlockSpec((FEAT, 2 * OWN), lambda j: (0, j)),
-            pl.BlockSpec((2 * OWN, FEAT), lambda j: (j, 0)),
+            pl.BlockSpec((FEAT, 512), lambda j: (0, j)),
+            pl.BlockSpec((512, FEAT), lambda j: (j, 0)),
         ],
         compiler_params=pltpu.CompilerParams(vmem_limit_bytes=60 * 2**20),
         cost_estimate=pl.CostEstimate(flops=3 * 10**9, bytes_accessed=18 * 2**20, transcendentals=0),

time: 129 us -> 120 us (0.930)
  the two profiles are of different devices: /device:TPU:59 before, /device:TPU:1 now
where the time goes in v3:
time: 120 us
  Pallas kernels  117 us (98%)
  between operations  2.39 us (2%)
    pallas_call x1, Pallas kernels, on_device(): pl.pallas_call(step_kernel, name='mlp_step', out_shape=[jax.ShapeDtypeStr...  107 us
    pallas_call x1, Pallas kernels, on_device(): pl.pallas_call(weight_kernel, name='weight_grads', grid=(HID // 512,), ou...  9.89 us

profile of v3, /device:TPU:1, one launch (start us, length us, event | category | flops | bytes accessed | tf_op | source)
XLA Modules:
  0.0 119.7 jit_solution(15630486620225646622)
XLA Ops:
  0.6 107.4 %mlp_step.1 = (bf16[384,1024]{1,0:T(8,128)(2,1)}, bf16[3072,1024]{1,0:T(8,128)(2,1)}, bf16[3072,256]{1,0:T(8,128)(2,1)}, f32[1,1]{1,0:T(1,128)}) custom-call(bf16[128,384]{1,0:T(8,128)(2,1)} %tok_hbm.1, f32[384]{0:T(512)} %gain_ref.1, bf16[384,3072]{1,0:T(8,128)(2,1)} %wup_hbm.1, bf16[3072,384]{1,0:T(8,128)(2,1)} %wdn_hbm.1, bf16[384,256]{1,0:T(8,128)(2,1)} %proj_ref.1, ...), custom_call_target="tpu_custom_call" | custom-call | flops 6000000000 | bytes 16777216 | tf_op jit(solution)/shard_map/mlp_step/pallas_call | solution.py:554
  108.0 9.9 %weight_grads.1 = (f32[384,3072]{1,0:T(8,128)}, f32[3072,384]{1,0:T(8,128)}) custom-call(bf16[384,1024]{1,0:T(8,128)(2,1)} %get-tuple-element.9.n_ref, bf16[3072,1024]{1,0:T(8,128)(2,1)} %get-tuple-element.10.gp_ref, bf16[3072,256]{1,0:T(8,128)(2,1)} %get-tuple-element.11.gh_ref, bf16[384,256]{1,0:T(8,128)(2,1)} %proj_ref.1), custom_call_target="tpu_custom_call" | custom-call | flops 3000000000 | bytes 18874368 | tf_op jit(solution)/shard_map/weight_grads/pallas_call | solution.py:626

commit v4 on v3

--- a/solution.py
+++ b/solution.py
@@ -23,7 +23,6 @@
 CH = 256
 TA = 512
 TB = TOK - TA
-GA = TA + CH
 FOCUS = 0.85
 EPS = 1e-06
 
@@ -59,7 +58,7 @@
     tok_ref, wup_ref, wdn, proj_ref, conv, depth_ref, mask_ref,
     xall, st_row, st_col, w_t, w_send, wd_peer, proj_peer, n_t, m_sum, m_part, m_recv, m_own,
     p_a, p_b, a1, a2, a3, b1, b2, b3, pre, hid, zc, z1, z1_recv, z2, z2_recv, z3,
-    taps, field, field_slope, shifted, pred_all, rows_buf, gz, ga, gb, gh_own, send_sems, recv_sems, local_sems, out_sems,
+    taps, field, field_slope, shifted, pred_all, rows_buf, gz, gm, ga, gb, gh_own, send_sems, recv_sems, local_sems, out_sems,
 ):
     row, col = lax.axis_index("row"), lax.axis_index("col")
     z, h, c = row // 4, lax.rem(row // 2, 2), lax.rem(row, 2)
@@ -140,33 +139,37 @@
     )
     own_half = pl.multiple_of(c * HALF, HALF)
     to_peer = pl.multiple_of(other * HALF, HALF)
+    pl.semaphore_wait(barrier, len(row_peers) + len(col_peers))
+
+    stat_copies = [remote(st_row.at[row], st_row.at[row], at_row(*peer)) for peer in row_peers]
+    across = remote(xall.at[col], xall.at[col], at_col(1, 0))
+    token_copies = [remote(xall.at[col], xall.at[col], at_col(0, dx)) for dx in (2, 1, 3)]
     proj_in.wait()
     wdn_copy.wait()
+    wd_copy = remote(wdn.at[pl.ds(to_peer, HALF)], wd_peer, partner)
+    proj_copy = remote(proj_ref, proj_peer, partner)
 
     @pl.loop(0, 8)
     def _(k):
         m_sum[k] = mm(wdn[pl.ds(pl.multiple_of(own_half + k * OWN, 64), OWN), :], proj_ref[...])
 
-    pl.semaphore_wait(barrier, len(row_peers) + len(col_peers))
-
-    stat_copies = [remote(st_row.at[row], st_row.at[row], at_row(*peer)) for peer in row_peers]
-    across = remote(xall.at[col], xall.at[col], at_col(1, 0))
-    token_copies = [remote(xall.at[col], xall.at[col], at_col(0, dx)) for dx in (2, 1, 3)]
-    wd_copy = remote(wdn.at[pl.ds(to_peer, HALF)], wd_peer, partner)
-    proj_copy = remote(proj_ref, proj_peer, partner)
-
-    feature_at = pl.multiple_of(c * FEAT, 128)
-    wup_copy.wait()
-
-    @pl.loop(0, HALF // 128)
-    def _(i):
-        at = pl.multiple_of(to_peer + i * 128, 128)
-        w_send[pl.ds(pl.multiple_of(i * 128, 128), 128), :] = wup_ref[:, pl.ds(at, 128)].T
-
     across.wait_recv()
     came = xall.at[lax.rem(col + 4, 8)]
     token_copies += [remote(came, came, at_col(0, dx)) for dx in (2, 1, 3)]
-    w_copy = remote(w_send, w_t.at[:, pl.ds(feature_at, FEAT)], partner)
+
+    wd_copy.wait_recv()
+    proj_copy.wait_recv()
+
+    @pl.loop(0, 8)
+    def _(k):
+        more = mm(wd_peer[pl.ds(pl.multiple_of(k * OWN, 64), OWN), :], proj_peer[...])
+        m_part[k] = (m_sum[k] + more).astype(BF16)
+
+    m_copies = []
+    for index, (dz, dh) in enumerate(chip_peers):
+        m_copies.append(
+            remote(m_part.at[zz(dz) * 2 + hh(dh)], m_recv.at[index], at_row(dz, dh, 0))
+        )
 
     for copy in stat_copies:
         copy.wait_recv()
@@ -191,19 +194,15 @@
     )
     norm_copies = [remote(st_col.at[col], st_col.at[col], at_col(*peer)) for peer in col_peers]
 
-    wd_copy.wait_recv()
-    proj_copy.wait_recv()
-
-    @pl.loop(0, 8)
-    def _(k):
-        more = mm(wd_peer[pl.ds(pl.multiple_of(k * OWN, 64), OWN), :], proj_peer[...])
-        m_part[k] = (m_sum[k] + more).astype(BF16)
-
-    m_copies = []
-    for index, (dz, dh) in enumerate(chip_peers):
-        m_copies.append(
-            remote(m_part.at[zz(dz) * 2 + hh(dh)], m_recv.at[index], at_row(dz, dh, 0))
-        )
+    feature_at = pl.multiple_of(c * FEAT, 128)
+    wup_copy.wait()
+
+    @pl.loop(0, HALF // 128)
+    def _(i):
+        at = pl.multiple_of(to_peer + i * 128, 128)
+        w_send[pl.ds(pl.multiple_of(i * 128, 128), 128), :] = wup_ref[:, pl.ds(at, 128)].T
+
+    w_copy = remote(w_send, w_t.at[:, pl.ds(feature_at, FEAT)], partner)
 
     @pl.loop(0, HALF // 128)
     def _(i):
@@ -293,7 +292,17 @@
     for index in range(7):
         total = total + m_recv[index].astype(F32)
     m_own[...] = total.astype(BF16)
-    ga[slot(0, 0), :, TA:] = m_own[...]
+    gm[slot(0, 0)] = m_own[...]
+    pair = []
+
+    def send(buf, dz, dh, device, rows=None):
+        ref = buf.at[slot(dz, dh)] if rows is None else buf.at[slot(dz, dh), rows[0] : rows[1]]
+        return remote(ref, ref, device)
+
+    mf = send(gm, 0, 0, flip)
+    mu = send(gm, 0, 0, up)
+    md = send(gm, 0, 0, down)
+    pair.append(send(gm, 0, 0, partner))
     x_proj = tn(proj_ref[...], xall[col])
 
     conv_copy.wait()
@@ -338,23 +347,16 @@
 
     bulk_from = len(sent)
     mine_a, mine_b = ga.at[slot(0, 0)], gb.at[slot(0, 0)]
-    pair = []
-
-    def send(buf, dz, dh, device, rows=None):
-        ref = buf.at[slot(dz, dh)] if rows is None else buf.at[slot(dz, dh), rows[0] : rows[1]]
-        return remote(ref, ref, device)
-
+    mf.wait_recv()
+    mfu = send(gm, 0, 1, up)
+    mfd = send(gm, 0, 1, down)
+    pair.append(send(gm, 0, 1, partner))
     top, low = (0, 96), (96, 192)
 
     @pl.loop(0, TB // 128)
     def _(t):
         at = pl.ds(pl.multiple_of(t * 128, 128), 128)
         mine_b[:, at] = slope(pre[:, pl.ds(pl.multiple_of(TA + t * 128, 128), 128)]).astype(BF16)
-
-    @pl.loop(0, TA // 128)
-    def _(t):
-        at = pl.ds(pl.multiple_of(t * 128, 128), 128)
-        mine_a[:, at] = slope(pre[:, at]).astype(BF16)
 
     z1_copy.wait_recv()
     z2[...] = (
@@ -366,8 +368,24 @@
         z2_copies.append(remote(z2.at[pl.ds(at, 16)], z2_recv.at[index], at_row(dz, dh, 0)))
     bu = send(gb, 0, 0, up)
     bd = send(gb, 0, 0, down)
+    mu.wait_recv()
+    mu2 = send(gm, 3, 0, up)
+    pair.append(send(gm, 3, 0, partner))
+    md.wait_recv()
+    pair.append(send(gm, 1, 0, partner))
+    pair.append(send(gb, 0, 0, partner))
+
+    @pl.loop(0, TA // 128)
+    def _(t):
+        at = pl.ds(pl.multiple_of(t * 128, 128), 128)
+        mine_a[:, at] = slope(pre[:, at]).astype(BF16)
+
     fa = send(ga, 0, 0, flip)
-    pair.append(send(gb, 0, 0, partner))
+    mfd.wait_recv()
+    mfd2 = send(gm, 1, 1, down)
+    pair.append(send(gm, 1, 1, partner))
+    mfu.wait_recv()
+    pair.append(send(gm, 3, 1, partner))
     pair.append(send(ga, 0, 0, partner))
     mine = pl.ds(pl.multiple_of(here * 16, 16), 16)
     part = z2[mine, :].astype(F32)
@@ -400,8 +418,17 @@
     fau = send(ga, 0, 1, up)
     fad = send(ga, 0, 1, down)
     pair.append(send(ga, 0, 1, partner))
+    au.wait_recv()
+    au2 = send(ga, 3, 0, up)
+    pair.append(send(ga, 3, 0, partner))
+    ad.wait_recv()
+    pair.append(send(ga, 1, 0, partner))
     fb.wait_recv()
     pair.append(send(gb, 0, 1, partner))
+    mu2.wait_recv()
+    pair.append(send(gm, 2, 0, partner))
+    mfd2.wait_recv()
+    pair.append(send(gm, 2, 1, partner))
     for copy in z4_copies:
         copy.wait_recv()
 
@@ -439,11 +466,6 @@
     bd2.wait_recv()
     f_low = send(gb, 2, 0, flip, low)
     pair.append(send(gb, 2, 0, partner, low))
-    au.wait_recv()
-    au2 = send(ga, 3, 0, up)
-    pair.append(send(ga, 3, 0, partner))
-    ad.wait_recv()
-    pair.append(send(ga, 1, 0, partner))
 
     @pl.loop(0, TOK // 128)
     def _(t):
@@ -518,10 +540,10 @@
 
     @pl.loop(0, 16)
     def _(k):
-        weights = ga[k, :, TA:]
-        ga[k, :, :TA] = (mm(weights, gz[:, :TA]) * ga[k, :, :TA].astype(F32)).astype(BF16)
+        weights = gm[k]
+        ga[k] = (mm(weights, gz[:, :TA]) * ga[k].astype(F32)).astype(BF16)
         gb[k] = (mm(weights, gz[:, TA:]) * gb[k].astype(F32)).astype(BF16)
-        pltpu.make_async_copy(ga.at[k, :, :TA], gp_out.at[pl.ds(pl.multiple_of(k * OWN, 64), OWN), :TA], out_sems.at[0, k]).start()
+        pltpu.make_async_copy(ga.at[k], gp_out.at[pl.ds(pl.multiple_of(k * OWN, 64), OWN), :TA], out_sems.at[0, k]).start()
         pltpu.make_async_copy(gb.at[k], gp_out.at[pl.ds(pl.multiple_of(k * OWN, 64), OWN), TA:], out_sems.at[1, k]).start()
 
     for (dz, dh), copy in zip(chip_peers, gh_copies):
@@ -533,7 +555,7 @@
 
     @pl.loop(0, 16)
     def _(k):
-        pltpu.make_async_copy(ga.at[k, :, :TA], gp_out.at[pl.ds(pl.multiple_of(k * OWN, 64), OWN), :TA], out_sems.at[0, k]).wait()
+        pltpu.make_async_copy(ga.at[k], gp_out.at[pl.ds(pl.multiple_of(k * OWN, 64), OWN), :TA], out_sems.at[0, k]).wait()
         pltpu.make_async_copy(gb.at[k], gp_out.at[pl.ds(pl.multiple_of(k * OWN, 64), OWN), TA:], out_sems.at[1, k]).wait()
 
     for copy in started[-2:]:
@@ -607,7 +629,8 @@
             pltpu.VMEM((2, 8, STRIP), F32),
             pltpu.VMEM((8, STRIP), F32),
             pltpu.VMEM((CH, TOK), BF16),
-            pltpu.VMEM((16, OWN, GA), BF16),
+            pltpu.VMEM((16, OWN, CH), BF16),
+            pltpu.VMEM((16, OWN, TA), BF16),
             pltpu.VMEM((16, OWN, TB), BF16),
             pltpu.VMEM((OWN, CH), BF16),
             pltpu.SemaphoreType.DMA((N_SEMS,)),

time: 120 us -> 119 us (level)
  no operation moved by 1% of the time
where the time goes in v4:
time: 119 us
  Pallas kernels  116 us (97%)
  between operations  2.39 us (2%)
    pallas_call x1, Pallas kernels, on_device(): pl.pallas_call(step_kernel, name='mlp_step', out_shape=[jax.ShapeDtypeStr...  106 us
    pallas_call x1, Pallas kernels, on_device(): pl.pallas_call(weight_kernel, name='weight_grads', grid=(HID // 512,), ou...  9.89 us

profile of v4, /device:TPU:1, one launch (start us, length us, event | category | flops | bytes accessed | tf_op | source)
XLA Modules:
  0.0 118.6 jit_solution(7924214900307569567)
XLA Ops:
  0.6 106.3 %mlp_step.1 = (bf16[384,1024]{1,0:T(8,128)(2,1)}, bf16[3072,1024]{1,0:T(8,128)(2,1)}, bf16[3072,256]{1,0:T(8,128)(2,1)}, f32[1,1]{1,0:T(1,128)}) custom-call(bf16[128,384]{1,0:T(8,128)(2,1)} %tok_hbm.1, f32[384]{0:T(512)} %gain_ref.1, bf16[384,3072]{1,0:T(8,128)(2,1)} %wup_hbm.1, bf16[3072,384]{1,0:T(8,128)(2,1)} %wdn_hbm.1, bf16[384,256]{1,0:T(8,128)(2,1)} %proj_ref.1, ...), custom_call_target="tpu_custom_call" | custom-call | flops 6000000000 | bytes 16777216 | tf_op jit(solution)/shard_map/mlp_step/pallas_call | solution.py:576
  106.9 9.9 %weight_grads.1 = (f32[384,3072]{1,0:T(8,128)}, f32[3072,384]{1,0:T(8,128)}) custom-call(bf16[384,1024]{1,0:T(8,128)(2,1)} %get-tuple-element.9.n_ref, bf16[3072,1024]{1,0:T(8,128)(2,1)} %get-tuple-element.10.gp_ref, bf16[3072,256]{1,0:T(8,128)(2,1)} %get-tuple-element.11.gh_ref, bf16[384,256]{1,0:T(8,128)(2,1)} %proj_ref.1), custom_call_target="tpu_custom_call" | custom-call | flops 3000000000 | bytes 18874368 | tf_op jit(solution)/shard_map/weight_grads/pallas_call | solution.py:649

commit v5 on v4

--- a/solution.py
+++ b/solution.py
@@ -54,11 +54,11 @@
 
 def step_kernel(
     tok_hbm, gain_ref, wup_hbm, wdn_hbm, proj_hbm, conv_hbm, head_ref, depth_hbm, mask_hbm,
-    nt_out, gp_out, gh_out, loss_ref,
+    up_out, gh_out, loss_ref,
     tok_ref, wup_ref, wdn, proj_ref, conv, depth_ref, mask_ref,
     xall, st_row, st_col, w_t, w_send, wd_peer, proj_peer, n_t, m_sum, m_part, m_recv, m_own,
     p_a, p_b, a1, a2, a3, b1, b2, b3, pre, hid, zc, z1, z1_recv, z2, z2_recv, z3,
-    taps, field, field_slope, shifted, pred_all, rows_buf, gz, gm, ga, gb, gh_own, send_sems, recv_sems, local_sems, out_sems,
+    taps, field, field_slope, shifted, pred_all, rows_buf, gz, gm, ga, gb, gh_own, grad, up_own, send_sems, recv_sems, local_sems, out_sems,
 ):
     row, col = lax.axis_index("row"), lax.axis_index("col")
     z, h, c = row // 4, lax.rem(row // 2, 2), lax.rem(row, 2)
@@ -224,7 +224,6 @@
             ).astype(BF16)
         half = n_t.at[pl.ds(feature_at, FEAT), first * STRIP : (first + 4) * STRIP]
         n_copies.append(remote(half, half, partner))
-    local(n_t.at[pl.ds(feature_at, FEAT)], nt_out)
     w_copy.wait_recv()
 
     a_copies, b_copies = {}, {}
@@ -293,16 +292,19 @@
         total = total + m_recv[index].astype(F32)
     m_own[...] = total.astype(BF16)
     gm[slot(0, 0)] = m_own[...]
-    pair = []
+    pair = {}
 
     def send(buf, dz, dh, device, rows=None):
         ref = buf.at[slot(dz, dh)] if rows is None else buf.at[slot(dz, dh), rows[0] : rows[1]]
         return remote(ref, ref, device)
 
+    def share(name, buf, dz, dh, rows=None):
+        pair[name] = send(buf, dz, dh, partner, rows)
+
     mf = send(gm, 0, 0, flip)
     mu = send(gm, 0, 0, up)
     md = send(gm, 0, 0, down)
-    pair.append(send(gm, 0, 0, partner))
+    share("gm00", gm, 0, 0)
     x_proj = tn(proj_ref[...], xall[col])
 
     conv_copy.wait()
@@ -345,12 +347,11 @@
     z1[...] = zc[pl.ds(pl.multiple_of(other * 128, 128), 128), :].astype(BF16)
     z1_copy = remote(z1, z1_recv, partner)
 
-    bulk_from = len(sent)
     mine_a, mine_b = ga.at[slot(0, 0)], gb.at[slot(0, 0)]
     mf.wait_recv()
     mfu = send(gm, 0, 1, up)
     mfd = send(gm, 0, 1, down)
-    pair.append(send(gm, 0, 1, partner))
+    share("gm01", gm, 0, 1)
     top, low = (0, 96), (96, 192)
 
     @pl.loop(0, TB // 128)
@@ -370,10 +371,10 @@
     bd = send(gb, 0, 0, down)
     mu.wait_recv()
     mu2 = send(gm, 3, 0, up)
-    pair.append(send(gm, 3, 0, partner))
+    share("gm30", gm, 3, 0)
     md.wait_recv()
-    pair.append(send(gm, 1, 0, partner))
-    pair.append(send(gb, 0, 0, partner))
+    share("gm10", gm, 1, 0)
+    share("gb00", gb, 0, 0)
 
     @pl.loop(0, TA // 128)
     def _(t):
@@ -383,10 +384,10 @@
     fa = send(ga, 0, 0, flip)
     mfd.wait_recv()
     mfd2 = send(gm, 1, 1, down)
-    pair.append(send(gm, 1, 1, partner))
+    share("gm11", gm, 1, 1)
     mfu.wait_recv()
-    pair.append(send(gm, 3, 1, partner))
-    pair.append(send(ga, 0, 0, partner))
+    share("gm31", gm, 3, 1)
+    share("ga00", ga, 0, 0)
     mine = pl.ds(pl.multiple_of(here * 16, 16), 16)
     part = z2[mine, :].astype(F32)
     for index, copy in enumerate(z2_copies):
@@ -399,10 +400,10 @@
     fb = send(gb, 0, 0, flip)
     bu.wait_recv()
     bu2 = send(gb, 3, 0, up, top)
-    pair.append(send(gb, 3, 0, partner))
+    share("gb30", gb, 3, 0)
     bd.wait_recv()
     bd2 = send(gb, 1, 0, down, low)
-    pair.append(send(gb, 1, 0, partner))
+    share("gb10", gb, 1, 0)
     for copy in z3_copies:
         copy.wait_recv()
     total = z3[0].astype(F32)
@@ -417,18 +418,24 @@
     fa.wait_recv()
     fau = send(ga, 0, 1, up)
     fad = send(ga, 0, 1, down)
-    pair.append(send(ga, 0, 1, partner))
+    share("ga01", ga, 0, 1)
     au.wait_recv()
     au2 = send(ga, 3, 0, up)
-    pair.append(send(ga, 3, 0, partner))
+    share("ga30", ga, 3, 0)
     ad.wait_recv()
-    pair.append(send(ga, 1, 0, partner))
+    share("ga10", ga, 1, 0)
     fb.wait_recv()
-    pair.append(send(gb, 0, 1, partner))
+    share("gb01", gb, 0, 1)
+    bu2.wait_recv()
+    f_top = send(gb, 2, 0, flip, top)
+    share("gb20top", gb, 2, 0, top)
+    bd2.wait_recv()
+    f_low = send(gb, 2, 0, flip, low)
+    share("gb20low", gb, 2, 0, low)
     mu2.wait_recv()
-    pair.append(send(gm, 2, 0, partner))
+    share("gm20", gm, 2, 0)
     mfd2.wait_recv()
-    pair.append(send(gm, 2, 1, partner))
+    share("gm21", gm, 2, 1)
     for copy in z4_copies:
         copy.wait_recv()
 
@@ -460,12 +467,6 @@
         rows_buf[index : index + 1, :] = pred[:, index * STRIP : (index + 1) * STRIP]
     pred_all[c] = rows_buf[...]
     pred_copy = remote(pred_all.at[c], pred_all.at[c], partner)
-    bu2.wait_recv()
-    f_top = send(gb, 2, 0, flip, top)
-    pair.append(send(gb, 2, 0, partner, top))
-    bd2.wait_recv()
-    f_low = send(gb, 2, 0, flip, low)
-    pair.append(send(gb, 2, 0, partner, low))
 
     @pl.loop(0, TOK // 128)
     def _(t):
@@ -509,42 +510,60 @@
         hid[...], gz[pl.ds(second_channel, 128), :]
     ).astype(BF16)
     local(gh_own, gh_out.at[own_rows(0, 0)])
-    bulk_to = len(sent)
     gh_copies = [
         remote(gh_own, gh_out.at[own_rows(0, 0)], at_row(dz, dh, 0)) for dz, dh in chip_peers
     ]
     gh_pair = [remote(gh_own, gh_out.at[own_rows(0, 0)], partner)]
-    bulk_end = len(sent)
-    f_m.wait_recv()
-    pair.append(send(gb, 3, 1, partner))
+    def ready(names):
+        for name in names.split():
+            pair[name].wait_recv()
+
+    n_mine = n_t.at[pl.ds(feature_at, FEAT)]
+
+    def column(dz):
+        @pl.loop(0, 2)
+        def _(core):
+            base = core * 8 + zz(dz) * 2
+            for half in (0, 1):
+                rows = slice(half * OWN, (half + 1) * OWN)
+                weights = gm[base + half]
+                grad[rows, :TA] = (
+                    mm(weights, gz[:, :TA]) * ga[base + half].astype(F32)
+                ).astype(BF16)
+                grad[rows, TA:] = (
+                    mm(weights, gz[:, TA:]) * gb[base + half].astype(F32)
+                ).astype(BF16)
+            up_own[dz, core] = nt(n_mine[...], grad[...])
+            at = pl.multiple_of(base * OWN, 2 * OWN)
+            pltpu.make_async_copy(
+                up_own.at[dz, core], up_out.at[:, pl.ds(at, 2 * OWN)], out_sems.at[dz, core]
+            ).start()
+
     fad.wait_recv()
     fad2 = send(ga, 1, 1, down)
-    pair.append(send(ga, 1, 1, partner))
+    share("ga11", ga, 1, 1)
     fau.wait_recv()
-    pair.append(send(ga, 3, 1, partner))
+    share("ga31", ga, 3, 1)
+    f_m.wait_recv()
+    share("gb31", gb, 3, 1)
     f_p.wait_recv()
-    pair.append(send(gb, 1, 1, partner))
+    share("gb11", gb, 1, 1)
+    ready("gm00 gb00 ga00 gm01 ga01 gb01")
+    column(0)
     f_top.wait_recv()
-    pair.append(send(gb, 2, 1, partner, top))
+    share("gb21top", gb, 2, 1, top)
     f_low.wait_recv()
-    pair.append(send(gb, 2, 1, partner, low))
+    share("gb21low", gb, 2, 1, low)
+    ready("gm30 gb30 ga30 gm31 ga31 gb31")
+    column(3)
     au2.wait_recv()
-    pair.append(send(ga, 2, 0, partner))
+    share("ga20", ga, 2, 0)
+    ready("gm10 gb10 ga10 gm11 ga11 gb11")
+    column(1)
     fad2.wait_recv()
-    pair.append(send(ga, 2, 1, partner))
-    for copy in pair:
-        copy.wait_recv()
-    bulk = sent[bulk_from:bulk_to] + sent[bulk_end:]
-    for copy in bulk:
-        copy.wait_send()
-
-    @pl.loop(0, 16)
-    def _(k):
-        weights = gm[k]
-        ga[k] = (mm(weights, gz[:, :TA]) * ga[k].astype(F32)).astype(BF16)
-        gb[k] = (mm(weights, gz[:, TA:]) * gb[k].astype(F32)).astype(BF16)
-        pltpu.make_async_copy(ga.at[k], gp_out.at[pl.ds(pl.multiple_of(k * OWN, 64), OWN), :TA], out_sems.at[0, k]).start()
-        pltpu.make_async_copy(gb.at[k], gp_out.at[pl.ds(pl.multiple_of(k * OWN, 64), OWN), TA:], out_sems.at[1, k]).start()
+    share("ga21", ga, 2, 1)
+    ready("gm20 gb20top gb20low ga20 gm21 ga21 gb21top gb21low")
+    column(2)
 
     for (dz, dh), copy in zip(chip_peers, gh_copies):
         copy.wait_recv()
@@ -553,39 +572,39 @@
     for copy in gh_pair:
         copy.wait_recv()
 
-    @pl.loop(0, 16)
-    def _(k):
-        pltpu.make_async_copy(ga.at[k], gp_out.at[pl.ds(pl.multiple_of(k * OWN, 64), OWN), :TA], out_sems.at[0, k]).wait()
-        pltpu.make_async_copy(gb.at[k], gp_out.at[pl.ds(pl.multiple_of(k * OWN, 64), OWN), TA:], out_sems.at[1, k]).wait()
-
-    for copy in started[-2:]:
-        copy.wait()
+    for dz in range(4):
+
+        @pl.loop(0, 2)
+        def _(core):
+            at = pl.multiple_of((core * 8 + zz(dz) * 2) * OWN, 2 * OWN)
+            pltpu.make_async_copy(
+                up_own.at[dz, core], up_out.at[:, pl.ds(at, 2 * OWN)], out_sems.at[dz, core]
+            ).wait()
+
+    started[-1].wait()
     for copy in sent:
-        if not any(copy is other_copy for other_copy in bulk):
-            copy.wait_send()
-
-
-def weight_kernel(n_ref, gp_ref, gh_ref, proj_ref, up_ref, down_ref):
-    up_ref[...] = nt(n_ref[...], gp_ref[...])
+        copy.wait_send()
+
+
+def weight_kernel(gh_ref, proj_ref, down_ref):
     down_ref[...] = nt(gh_ref[...], proj_ref[...])
 
 
 def on_device(tokens, ln_gain, w_up, w_down, proj, conv_kernel, head_weight, depth_mm, lidar_mask):
     vmem = pl.BlockSpec(memory_space=pltpu.VMEM)
     anywhere = pl.BlockSpec(memory_space=pl.ANY)
-    normed, grad_pre, grad_hidden, loss = pl.pallas_call(
+    grad_up, grad_hidden, loss = pl.pallas_call(
         step_kernel,
         name="mlp_step",
         out_shape=[
-            jax.ShapeDtypeStruct((FEAT, TOK), BF16),
-            jax.ShapeDtypeStruct((HID, TOK), BF16),
+            jax.ShapeDtypeStruct((FEAT, HID), F32),
             jax.ShapeDtypeStruct((HID, CH), BF16),
             jax.ShapeDtypeStruct((1, 1), F32),
         ],
         in_specs=[
             anywhere, vmem, anywhere, anywhere, anywhere, anywhere, vmem, anywhere, anywhere,
         ],
-        out_specs=[anywhere, anywhere, anywhere, pl.BlockSpec(memory_space=pltpu.SMEM)],
+        out_specs=[anywhere, anywhere, pl.BlockSpec(memory_space=pltpu.SMEM)],
         scratch_shapes=[
             pltpu.VMEM((STRIP, FEAT), BF16),
             pltpu.VMEM((FEAT, HID), BF16),
@@ -633,10 +652,12 @@
             pltpu.VMEM((16, OWN, TA), BF16),
             pltpu.VMEM((16, OWN, TB), BF16),
             pltpu.VMEM((OWN, CH), BF16),
+            pltpu.VMEM((2 * OWN, TOK), BF16),
+            pltpu.VMEM((4, 2, FEAT, 2 * OWN), F32),
             pltpu.SemaphoreType.DMA((N_SEMS,)),
             pltpu.SemaphoreType.DMA((N_SEMS,)),
             pltpu.SemaphoreType.DMA((9,)),
-            pltpu.SemaphoreType.DMA((2, 16)),
+            pltpu.SemaphoreType.DMA((4, 2)),
         ],
         compiler_params=pltpu.CompilerParams(
             collective_id=0, has_side_effects=True, vmem_limit_bytes=60 * 2**20
@@ -646,27 +667,19 @@
         tokens, ln_gain, w_up, w_down, proj, conv_kernel.reshape(9, CH, CH),
         head_weight.reshape(1, CH), depth_mm, lidar_mask,
     )
-    grad_up, grad_down = pl.pallas_call(
+    grad_down = pl.pallas_call(
         weight_kernel,
         name="weight_grads",
         grid=(HID // 512,),
-        out_shape=[
-            jax.ShapeDtypeStruct((FEAT, HID), F32),
-            jax.ShapeDtypeStruct((HID, FEAT), F32),
-        ],
+        out_shape=jax.ShapeDtypeStruct((HID, FEAT), F32),
         in_specs=[
-            pl.BlockSpec((FEAT, TOK), lambda j: (0, 0)),
-            pl.BlockSpec((512, TOK), lambda j: (j, 0)),
             pl.BlockSpec((512, CH), lambda j: (j, 0)),
             pl.BlockSpec((FEAT, CH), lambda j: (0, 0)),
         ],
-        out_specs=[
-            pl.BlockSpec((FEAT, 512), lambda j: (0, j)),
-            pl.BlockSpec((512, FEAT), lambda j: (j, 0)),
-        ],
+        out_specs=pl.BlockSpec((512, FEAT), lambda j: (j, 0)),
         compiler_params=pltpu.CompilerParams(vmem_limit_bytes=60 * 2**20),
-        cost_estimate=pl.CostEstimate(flops=3 * 10**9, bytes_accessed=18 * 2**20, transcendentals=0),
-    )(normed, grad_pre, grad_hidden, proj)
+        cost_estimate=pl.CostEstimate(flops=6 * 10**8, bytes_accessed=6 * 2**20, transcendentals=0),
+    )(grad_hidden, proj)
     return (grad_up, grad_down, loss.reshape(()))
 
 

time: 119 us -> 117 us (0.983)
  Pallas kernels: 116 us -> 109 us
  local copies, waits for them, and re-layouts: 0 us -> 5.05 us
    unnamed x0 -> x1, local copies, waits for them, and re-layouts: none -> 5.05 us
    pallas_call x1, Pallas kernels: 9.89 us -> 5.97 us  [on_device(): pl.pallas_call(weight_kernel, name='weight_grads', grid=(HID // 512,), ou...]
    pallas_call x1, Pallas kernels: 106 us -> 103 us  [on_device(): pl.pallas_call(step_kernel, name='mlp_step', out_shape=[jax.ShapeDtypeStr...]
where the time goes in v5:
time: 117 us
  Pallas kernels  109 us (93%)
  local copies, waits for them, and re-layouts  5.05 us (4%)
  between operations  2.41 us (2%)
    pallas_call x1, Pallas kernels, on_device(): pl.pallas_call(step_kernel, name='mlp_step', out_shape=[jax.ShapeDtypeStr...  103 us
    pallas_call x1, Pallas kernels, on_device(): pl.pallas_call(weight_kernel, name='weight_grads', grid=(HID // 512,), ou...  5.97 us
    unnamed x1, local copies, waits for them, and re-layouts  5.05 us

profile of v5, /device:TPU:1, one launch (start us, length us, event | category | flops | bytes accessed | tf_op | source)
XLA Modules:
  0.0 116.7 jit_solution(13809015449252361815)
XLA Ops:
  0.6 103.2 %mlp_step.1 = (f32[384,3072]{1,0:T(8,128)}, bf16[3072,256]{1,0:T(8,128)(2,1)}, f32[1,1]{1,0:T(1,128)}) custom-call(bf16[128,384]{1,0:T(8,128)(2,1)} %tok_hbm.1, f32[384]{0:T(512)} %gain_ref.1, bf16[384,3072]{1,0:T(8,128)(2,1)} %wup_hbm.1, bf16[3072,384]{1,0:T(8,128)(2,1)} %wdn_hbm.1, bf16[384,256]{1,0:T(8,128)(2,1)} %proj_ref.1, ...), custom_call_target="tpu_custom_call" | custom-call | flops 6000000000 | bytes 16777216 | tf_op jit(solution)/shard_map/mlp_step/pallas_call | solution.py:596
  103.9 6.0 %weight_grads.1 = f32[3072,384]{1,0:T(8,128)} custom-call(bf16[3072,256]{1,0:T(8,128)(2,1)} %get-tuple-element.7.gh_ref, bf16[384,256]{1,0:T(8,128)(2,1)} %proj_ref.1), custom_call_target="tpu_custom_call" | custom-call | flops 600000000 | bytes 6291456 | tf_op jit(solution)/shard_map/weight_grads/pallas_call | solution.py:670
  109.8 5.1 %copy.14 = f32[384,3072]{1,0:T(8,128)} copy(f32[384,3072]{1,0:T(8,128)} %get-tuple-element.12) | data formatting | bytes 9437184

commit v6 on v5

--- a/solution.py
+++ b/solution.py
@@ -30,6 +30,8 @@
 DENSITY = 1.0 / math.sqrt(2.0 * math.pi)
 
 N_SEMS = 192
+N_DOWN = 6
+N_UP = 8
 
 
 def cdf(v):
@@ -304,7 +306,7 @@
     mf = send(gm, 0, 0, flip)
     mu = send(gm, 0, 0, up)
     md = send(gm, 0, 0, down)
-    share("gm00", gm, 0, 0)
+    share(("gm", 0, 0, ""), gm, 0, 0)
     x_proj = tn(proj_ref[...], xall[col])
 
     conv_copy.wait()
@@ -351,7 +353,7 @@
     mf.wait_recv()
     mfu = send(gm, 0, 1, up)
     mfd = send(gm, 0, 1, down)
-    share("gm01", gm, 0, 1)
+    share(("gm", 0, 1, ""), gm, 0, 1)
     top, low = (0, 96), (96, 192)
 
     @pl.loop(0, TB // 128)
@@ -371,10 +373,10 @@
     bd = send(gb, 0, 0, down)
     mu.wait_recv()
     mu2 = send(gm, 3, 0, up)
-    share("gm30", gm, 3, 0)
+    share(("gm", 3, 0, ""), gm, 3, 0)
     md.wait_recv()
-    share("gm10", gm, 1, 0)
-    share("gb00", gb, 0, 0)
+    share(("gm", 1, 0, ""), gm, 1, 0)
+    share(("gb", 0, 0, ""), gb, 0, 0)
 
     @pl.loop(0, TA // 128)
     def _(t):
@@ -384,10 +386,10 @@
     fa = send(ga, 0, 0, flip)
     mfd.wait_recv()
     mfd2 = send(gm, 1, 1, down)
-    share("gm11", gm, 1, 1)
+    share(("gm", 1, 1, ""), gm, 1, 1)
     mfu.wait_recv()
-    share("gm31", gm, 3, 1)
-    share("ga00", ga, 0, 0)
+    share(("gm", 3, 1, ""), gm, 3, 1)
+    share(("ga", 0, 0, ""), ga, 0, 0)
     mine = pl.ds(pl.multiple_of(here * 16, 16), 16)
     part = z2[mine, :].astype(F32)
     for index, copy in enumerate(z2_copies):
@@ -400,10 +402,10 @@
     fb = send(gb, 0, 0, flip)
     bu.wait_recv()
     bu2 = send(gb, 3, 0, up, top)
-    share("gb30", gb, 3, 0)
+    share(("gb", 3, 0, ""), gb, 3, 0)
     bd.wait_recv()
     bd2 = send(gb, 1, 0, down, low)
-    share("gb10", gb, 1, 0)
+    share(("gb", 1, 0, ""), gb, 1, 0)
     for copy in z3_copies:
         copy.wait_recv()
     total = z3[0].astype(F32)
@@ -418,24 +420,24 @@
     fa.wait_recv()
     fau = send(ga, 0, 1, up)
     fad = send(ga, 0, 1, down)
-    share("ga01", ga, 0, 1)
+    share(("ga", 0, 1, ""), ga, 0, 1)
     au.wait_recv()
     au2 = send(ga, 3, 0, up)
-    share("ga30", ga, 3, 0)
+    share(("ga", 3, 0, ""), ga, 3, 0)
     ad.wait_recv()
-    share("ga10", ga, 1, 0)
+    share(("ga", 1, 0, ""), ga, 1, 0)
     fb.wait_recv()
-    share("gb01", gb, 0, 1)
+    share(("gb", 0, 1, ""), gb, 0, 1)
     bu2.wait_recv()
     f_top = send(gb, 2, 0, flip, top)
-    share("gb20top", gb, 2, 0, top)
+    share(("gb", 2, 0, "top"), gb, 2, 0, top)
     bd2.wait_recv()
     f_low = send(gb, 2, 0, flip, low)
-    share("gb20low", gb, 2, 0, low)
+    share(("gb", 2, 0, "low"), gb, 2, 0, low)
     mu2.wait_recv()
-    share("gm20", gm, 2, 0)
+    share(("gm", 2, 0, ""), gm, 2, 0)
     mfd2.wait_recv()
-    share("gm21", gm, 2, 1)
+    share(("gm", 2, 1, ""), gm, 2, 1)
     for copy in z4_copies:
         copy.wait_recv()
 
@@ -514,9 +516,10 @@
         remote(gh_own, gh_out.at[own_rows(0, 0)], at_row(dz, dh, 0)) for dz, dh in chip_peers
     ]
     gh_pair = [remote(gh_own, gh_out.at[own_rows(0, 0)], partner)]
-    def ready(names):
-        for name in names.split():
-            pair[name].wait_recv()
+    def ready(dz):
+        for key, copy in pair.items():
+            if key[1] == dz:
+                copy.wait_recv()
 
     n_mine = n_t.at[pl.ds(feature_at, FEAT)]
 
@@ -541,28 +544,28 @@
 
     fad.wait_recv()
     fad2 = send(ga, 1, 1, down)
-    share("ga11", ga, 1, 1)
+    share(("ga", 1, 1, ""), ga, 1, 1)
     fau.wait_recv()
-    share("ga31", ga, 3, 1)
+    share(("ga", 3, 1, ""), ga, 3, 1)
     f_m.wait_recv()
-    share("gb31", gb, 3, 1)
+    share(("gb", 3, 1, ""), gb, 3, 1)
     f_p.wait_recv()
-    share("gb11", gb, 1, 1)
-    ready("gm00 gb00 ga00 gm01 ga01 gb01")
+    share(("gb", 1, 1, ""), gb, 1, 1)
+    ready(0)
     column(0)
     f_top.wait_recv()
-    share("gb21top", gb, 2, 1, top)
+    share(("gb", 2, 1, "top"), gb, 2, 1, top)
     f_low.wait_recv()
-    share("gb21low", gb, 2, 1, low)
-    ready("gm30 gb30 ga30 gm31 ga31 gb31")
+    share(("gb", 2, 1, "low"), gb, 2, 1, low)
+    ready(3)
     column(3)
     au2.wait_recv()
-    share("ga20", ga, 2, 0)
-    ready("gm10 gb10 ga10 gm11 ga11 gb11")
+    share(("ga", 2, 0, ""), ga, 2, 0)
+    ready(1)
     column(1)
     fad2.wait_recv()
-    share("ga21", ga, 2, 1)
-    ready("gm20 gb20top gb20low ga20 gm21 ga21 gb21top gb21low")
+    share(("ga", 2, 1, ""), ga, 2, 1)
+    ready(2)
     column(2)
 
     for (dz, dh), copy in zip(chip_peers, gh_copies):
@@ -586,14 +589,49 @@
         copy.wait_send()
 
 
-def weight_kernel(gh_ref, proj_ref, down_ref):
-    down_ref[...] = nt(gh_ref[...], proj_ref[...])
+def weight_kernel(gh_hbm, proj_hbm, up_hbm, up_out, down_out, gh, proj, up, down, in_sems, out_sems):
+    rows, lines = HID // N_DOWN, FEAT // N_UP
+
+    def down_at(index):
+        return pl.ds(index * rows, rows)
+
+    def up_at(index):
+        return pl.ds(index * lines, lines)
+
+    proj_in = pltpu.make_async_copy(proj_hbm, proj, in_sems.at[0])
+    gh_in = [
+        pltpu.make_async_copy(gh_hbm.at[down_at(k)], gh.at[down_at(k)], in_sems.at[1 + k])
+        for k in range(N_DOWN)
+    ]
+    up_in = [
+        pltpu.make_async_copy(up_hbm.at[up_at(k)], up.at[up_at(k)], in_sems.at[1 + N_DOWN + k])
+        for k in range(N_UP)
+    ]
+    for copy in [proj_in] + gh_in + up_in:
+        copy.start()
+    leaving = []
+    proj_in.wait()
+    for k in range(N_DOWN):
+        gh_in[k].wait()
+        down[down_at(k), :] = nt(gh[down_at(k), :], proj[...])
+        leaving.append(
+            pltpu.make_async_copy(down.at[down_at(k)], down_out.at[down_at(k)], out_sems.at[k])
+        )
+        leaving[-1].start()
+    for k in range(N_UP):
+        up_in[k].wait()
+        leaving.append(
+            pltpu.make_async_copy(up.at[up_at(k)], up_out.at[up_at(k)], out_sems.at[N_DOWN + k])
+        )
+        leaving[-1].start()
+    for copy in leaving:
+        copy.wait()
 
 
 def on_device(tokens, ln_gain, w_up, w_down, proj, conv_kernel, head_weight, depth_mm, lidar_mask):
     vmem = pl.BlockSpec(memory_space=pltpu.VMEM)
     anywhere = pl.BlockSpec(memory_space=pl.ANY)
-    grad_up, grad_hidden, loss = pl.pallas_call(
+    up_held, grad_hidden, loss = pl.pallas_call(
         step_kernel,
         name="mlp_step",
         out_shape=[
@@ -667,19 +705,26 @@
         tokens, ln_gain, w_up, w_down, proj, conv_kernel.reshape(9, CH, CH),
         head_weight.reshape(1, CH), depth_mm, lidar_mask,
     )
-    grad_down = pl.pallas_call(
+    grad_up, grad_down = pl.pallas_call(
         weight_kernel,
         name="weight_grads",
-        grid=(HID // 512,),
-        out_shape=jax.ShapeDtypeStruct((HID, FEAT), F32),
-        in_specs=[
-            pl.BlockSpec((512, CH), lambda j: (j, 0)),
-            pl.BlockSpec((FEAT, CH), lambda j: (0, 0)),
+        out_shape=[
+            jax.ShapeDtypeStruct((FEAT, HID), F32),
+            jax.ShapeDtypeStruct((HID, FEAT), F32),
         ],
-        out_specs=pl.BlockSpec((512, FEAT), lambda j: (j, 0)),
+        in_specs=[anywhere, anywhere, anywhere],
+        out_specs=[anywhere, anywhere],
+        scratch_shapes=[
+            pltpu.VMEM((HID, CH), BF16),
+            pltpu.VMEM((FEAT, CH), BF16),
+            pltpu.VMEM((FEAT, HID), F32),
+            pltpu.VMEM((HID, FEAT), F32),
+            pltpu.SemaphoreType.DMA((1 + N_DOWN + N_UP,)),
+            pltpu.SemaphoreType.DMA((N_DOWN + N_UP,)),
+        ],
         compiler_params=pltpu.CompilerParams(vmem_limit_bytes=60 * 2**20),
-        cost_estimate=pl.CostEstimate(flops=6 * 10**8, bytes_accessed=6 * 2**20, transcendentals=0),
-    )(grad_hidden, proj)
+        cost_estimate=pl.CostEstimate(flops=6 * 10**8, bytes_accessed=16 * 2**20, transcendentals=0),
+    )(grad_hidden, proj, up_held)
     return (grad_up, grad_down, loss.reshape(()))
 
 

time: 117 us -> 111 us (0.949)
  local copies, waits for them, and re-layouts: 5.05 us -> 0 us
    unnamed x1 -> x0, local copies, waits for them, and re-layouts: 5.05 us -> none
where the time goes in v6:
time: 111 us
  Pallas kernels  109 us (98%)
  between operations  2.4 us (2%)
    pallas_call x1, Pallas kernels, on_device(): pl.pallas_call(step_kernel, name='mlp_step', out_shape=[jax.ShapeDtypeStr...  103 us
    pallas_call x1, Pallas kernels, on_device(): pl.pallas_call(weight_kernel, name='weight_grads', out_shape=[jax.ShapeDt...  5.59 us

profile of v6, /device:TPU:1, one launch (start us, length us, event | category | flops | bytes accessed | tf_op | source)
XLA Modules:
  0.0 111.2 jit_solution(6906572053027192659)
XLA Ops:
  0.6 103.2 %mlp_step.1 = (f32[384,3072]{1,0:T(8,128)}, bf16[3072,256]{1,0:T(8,128)(2,1)}, f32[1,1]{1,0:T(1,128)}) custom-call(bf16[128,384]{1,0:T(8,128)(2,1)} %tok_hbm.1, f32[384]{0:T(512)} %gain_ref.1, bf16[384,3072]{1,0:T(8,128)(2,1)} %wup_hbm.1, bf16[3072,384]{1,0:T(8,128)(2,1)} %wdn_hbm.1, bf16[384,256]{1,0:T(8,128)(2,1)} %proj_hbm.3, ...), custom_call_target="tpu_custom_call" | custom-call | flops 6000000000 | bytes 16777216 | tf_op jit(solution)/shard_map/mlp_step/pallas_call | solution.py:634
  103.9 5.6 %weight_grads.1 = (f32[384,3072]{1,0:T(8,128)}, f32[3072,384]{1,0:T(8,128)}) custom-call(bf16[3072,256]{1,0:T(8,128)(2,1)} %get-tuple-element.8.gh_hbm, bf16[384,256]{1,0:T(8,128)(2,1)} %proj_hbm.3, f32[384,3072]{1,0:T(8,128)} %get-tuple-element.9.up_hbm), custom_call_target="tpu_custom_call" | custom-call | flops 600000000 | bytes 16777216 | tf_op jit(solution)/shard_map/weight_grads/pallas_call | solution.py:708

commit v7 on v6

--- a/solution.py
+++ b/solution.py
@@ -248,21 +248,29 @@
     a_up = remote(p_a.at[zz(2), 0], a1.at[0], up)
     a_down = remote(p_a.at[zz(2), 1], a1.at[1], down)
     n_copies[1].wait_recv()
-    for dz in (2, 1, 3, 0):
+
+    def project_b(dz):
         project(dz, p_b, TA)
         b_copies[dz] = remote(p_b.at[zz(dz), 1 - h], b1.at[zz(dz)], flip)
+
+    project_b(2)
+    project(1, p_a, 0)
+    a_up1 = remote(p_a.at[zz(1), 1], a2.at[0, 1], up)
+    project(3, p_a, 0)
+    a_down1 = remote(p_a.at[zz(3), 0], a2.at[1, 0], down)
     for dz in (1, 3, 0):
-        project(dz, p_a, 0)
+        project_b(dz)
+    project(0, p_a, 0)
 
     def add(into, more):
         into[...] = (into[...].astype(F32) + more[...].astype(F32)).astype(BF16)
 
     a_up.wait_recv()
     add(p_a.at[zz(1), 0], a1.at[0])
-    a_up2 = remote(p_a.at[zz(1)], a2.at[0], up)
+    a_up2 = remote(p_a.at[zz(1), 0], a2.at[0, 0], up)
     a_down.wait_recv()
     add(p_a.at[zz(3), 1], a1.at[1])
-    a_down2 = remote(p_a.at[zz(3)], a2.at[1], down)
+    a_down2 = remote(p_a.at[zz(3), 1], a2.at[1, 1], down)
 
     b_copies[2].wait_recv()
     add(p_b.at[zz(2), h], b1.at[zz(2)])
@@ -273,8 +281,8 @@
     b_copies[3].wait_recv()
     add(p_b.at[zz(3), h], b1.at[zz(3)])
 
-    a_up2.wait_recv()
-    a_down2.wait_recv()
+    for copy in (a_up1, a_down1, a_up2, a_down2):
+        copy.wait_recv()
     p_a[z, 1 - h] = (
         p_a[z, 1 - h].astype(F32) + a2[0, 1 - h].astype(F32) + a2[1, 1 - h].astype(F32)
     ).astype(BF16)
@@ -469,6 +477,11 @@
         rows_buf[index : index + 1, :] = pred[:, index * STRIP : (index + 1) * STRIP]
     pred_all[c] = rows_buf[...]
     pred_copy = remote(pred_all.at[c], pred_all.at[c], partner)
+    fad.wait_recv()
+    fad2 = send(ga, 1, 1, down)
+    share(("ga", 1, 1, ""), ga, 1, 1)
+    fau.wait_recv()
+    share(("ga", 3, 1, ""), ga, 3, 1)
 
     @pl.loop(0, TOK // 128)
     def _(t):
@@ -542,11 +555,6 @@
                 up_own.at[dz, core], up_out.at[:, pl.ds(at, 2 * OWN)], out_sems.at[dz, core]
             ).start()
 
-    fad.wait_recv()
-    fad2 = send(ga, 1, 1, down)
-    share(("ga", 1, 1, ""), ga, 1, 1)
-    fau.wait_recv()
-    share(("ga", 3, 1, ""), ga, 3, 1)
     f_m.wait_recv()
     share(("gb", 3, 1, ""), gb, 3, 1)
     f_p.wait_recv()

time: 111 us -> 109 us (0.982)
  Pallas kernels: 109 us -> 106 us
    pallas_call x1, Pallas kernels: 103 us -> 100 us  [on_device(): pl.pallas_call(step_kernel, name='mlp_step', out_shape=[jax.ShapeDtypeStr...]
where the time goes in v7:
time: 109 us; the launch traced here: 108 us
  Pallas kernels  106 us (97%)
  between operations  2.4 us (2%)
    pallas_call x1, Pallas kernels, on_device(): pl.pallas_call(step_kernel, name='mlp_step', out_shape=[jax.ShapeDtypeStr...  100 us
    pallas_call x1, Pallas kernels, on_device(): pl.pallas_call(weight_kernel, name='weight_grads', out_shape=[jax.ShapeDt...  5.6 us

profile of v7, /device:TPU:1, one launch (start us, length us, event | category | flops | bytes accessed | tf_op | source)
XLA Modules:
  0.0 108.4 jit_solution(3425067234867880456)
XLA Ops:
  0.6 100.4 %mlp_step.1 = (f32[384,3072]{1,0:T(8,128)}, bf16[3072,256]{1,0:T(8,128)(2,1)}, f32[1,1]{1,0:T(1,128)}) custom-call(bf16[128,384]{1,0:T(8,128)(2,1)} %tok_hbm.1, f32[384]{0:T(512)} %gain_ref.1, bf16[384,3072]{1,0:T(8,128)(2,1)} %wup_hbm.1, bf16[3072,384]{1,0:T(8,128)(2,1)} %wdn_hbm.1, bf16[384,256]{1,0:T(8,128)(2,1)} %proj_hbm.3, ...), custom_call_target="tpu_custom_call" | custom-call | flops 6000000000 | bytes 16777216 | tf_op jit(solution)/shard_map/mlp_step/pallas_call | solution.py:642
  101.1 5.6 %weight_grads.1 = (f32[384,3072]{1,0:T(8,128)}, f32[3072,384]{1,0:T(8,128)}) custom-call(bf16[3072,256]{1,0:T(8,128)(2,1)} %get-tuple-element.8.gh_hbm, bf16[384,256]{1,0:T(8,128)(2,1)} %proj_hbm.3, f32[384,3072]{1,0:T(8,128)} %get-tuple-element.9.up_hbm), custom_call_target="tpu_custom_call" | custom-call | flops 600000000 | bytes 16777216 | tf_op jit(solution)/shard_map/weight_grads/pallas_call | solution.py:716

commit v8 on v7

--- a/solution.py
+++ b/solution.py
@@ -315,7 +315,8 @@
     mu = send(gm, 0, 0, up)
     md = send(gm, 0, 0, down)
     share(("gm", 0, 0, ""), gm, 0, 0)
-    x_proj = tn(proj_ref[...], xall[col])
+    zc[...] = jnp.zeros_like(zc)
+    zc[:, pl.ds(pl.multiple_of(col * STRIP, STRIP), STRIP)] = tn(proj_ref[...], xall[col])
 
     conv_copy.wait()
     head = head_ref[...]
@@ -329,106 +330,120 @@
         jnp.sum(jnp.where(lane == sub + first_channel, head, 0.0), axis=1, keepdims=True), (128, 128)
     )
 
-    b_copies[0].wait_recv()
+    lanes = (slice(0, TA), slice(TA, TOK))
+    mine = pl.ds(pl.multiple_of(here * 16, 16), 16)
+    mine_a, mine_b = ga.at[slot(0, 0)], gb.at[slot(0, 0)]
+    top, low = (0, 96), (96, 192)
+
+    def hidden(part):
+        @pl.loop(0, TA // 256)
+        def _(t):
+            at = pl.ds(pl.multiple_of(part * TA + t * 256, 256), 256)
+            value = pre[:, at]
+            value = (value * cdf(value)).astype(BF16)
+            hid[:, at] = value
+            zc[:, at] = zc[:, at] + tn(m_own[...], value)
+
+        at = lanes[part]
+        z1[:, at] = zc[pl.ds(pl.multiple_of(other * 128, 128), 128), at].astype(BF16)
+        return remote(z1.at[:, at], z1_recv.at[:, at], partner)
+
+    def steep(part, into):
+        @pl.loop(0, TA // 128)
+        def _(t):
+            at = pl.ds(pl.multiple_of(t * 128, 128), 128)
+            into[:, at] = slope(
+                pre[:, pl.ds(pl.multiple_of(part * TA + t * 128, 128), 128)]
+            ).astype(BF16)
+
+    def over_row(part, copy):
+        at = lanes[part]
+        copy.wait_recv()
+        z2[:, at] = (
+            zc[pl.ds(pl.multiple_of(c * 128, 128), 128), at] + z1_recv[:, at].astype(F32)
+        ).astype(BF16)
+        copies = []
+        for index, (dz, dh) in enumerate(chip_peers):
+            rows = pl.ds(pl.multiple_of((zz(dz) * 2 + hh(dh)) * 16, 16), 16)
+            copies.append(remote(z2.at[rows, at], z2_recv.at[index, :, at], at_row(dz, dh, 0)))
+        return copies
+
+    def over_col(part, copies):
+        at = lanes[part]
+        total = z2[mine, at].astype(F32)
+        for index, copy in enumerate(copies):
+            copy.wait_recv()
+            total = total + z2_recv[index, :, at].astype(F32)
+        z3[col, :, at] = total.astype(BF16)
+        return [remote(z3.at[col, :, at], z3.at[col, :, at], at_col(*peer)) for peer in col_peers]
+
+    def to_row(part, copies):
+        at = lanes[part]
+        for copy in copies:
+            copy.wait_recv()
+        total = z3[0, :, at].astype(F32)
+        for index in range(1, 8):
+            total = total + z3[index, :, at].astype(F32)
+        field[mine, at] = total.astype(BF16)
+        return [
+            remote(field.at[mine, at], field.at[mine, at], at_row(dz, dh, 0)) for dz, dh in chip_peers
+        ]
+
     a_flip.wait_recv()
     pre[:, :TA] = (
         p_a[z, h].astype(F32) + a2[0, h].astype(F32) + a2[1, h].astype(F32) + a3[...].astype(F32)
     )
+    z1_a = hidden(0)
+    steep(0, mine_a)
+    z2_a = over_row(0, z1_a)
+    fa = send(ga, 0, 0, flip)
+    au = send(ga, 0, 0, up)
+    ad = send(ga, 0, 0, down)
+    share(("ga", 0, 0, ""), ga, 0, 0)
+
+    b_copies[0].wait_recv()
     b_up2.wait_recv()
     b_down2.wait_recv()
     pre[:, TA:] = (
         p_b[z, h].astype(F32) + b1[z].astype(F32) + b3[0].astype(F32) + b3[1].astype(F32)
     )
-
-    @pl.loop(0, TOK // 128)
-    def _(t):
-        at = pl.ds(pl.multiple_of(t * 128, 128), 128)
-        value = pre[:, at]
-        hid[:, at] = (value * cdf(value)).astype(BF16)
-
-    @pl.loop(0, TOK // 256)
-    def _(t):
-        at = pl.ds(pl.multiple_of(t * 256, 256), 256)
-        zc[:, at] = tn(m_own[...], hid[:, at])
-
-    strip = pl.ds(pl.multiple_of(col * STRIP, STRIP), STRIP)
-    zc[:, strip] = zc[:, strip] + x_proj
-
-    z1[...] = zc[pl.ds(pl.multiple_of(other * 128, 128), 128), :].astype(BF16)
-    z1_copy = remote(z1, z1_recv, partner)
-
-    mine_a, mine_b = ga.at[slot(0, 0)], gb.at[slot(0, 0)]
+    z1_b = hidden(1)
+    z3_a = over_col(0, z2_a)
+    steep(1, mine_b)
+    z2_b = over_row(1, z1_b)
+    bu = send(gb, 0, 0, up)
+    bd = send(gb, 0, 0, down)
+    share(("gb", 0, 0, ""), gb, 0, 0)
     mf.wait_recv()
     mfu = send(gm, 0, 1, up)
     mfd = send(gm, 0, 1, down)
     share(("gm", 0, 1, ""), gm, 0, 1)
-    top, low = (0, 96), (96, 192)
-
-    @pl.loop(0, TB // 128)
-    def _(t):
-        at = pl.ds(pl.multiple_of(t * 128, 128), 128)
-        mine_b[:, at] = slope(pre[:, pl.ds(pl.multiple_of(TA + t * 128, 128), 128)]).astype(BF16)
-
-    z1_copy.wait_recv()
-    z2[...] = (
-        zc[pl.ds(pl.multiple_of(c * 128, 128), 128), :] + z1_recv[...].astype(F32)
-    ).astype(BF16)
-    z2_copies = []
-    for index, (dz, dh) in enumerate(chip_peers):
-        at = pl.multiple_of((zz(dz) * 2 + hh(dh)) * 16, 16)
-        z2_copies.append(remote(z2.at[pl.ds(at, 16)], z2_recv.at[index], at_row(dz, dh, 0)))
-    bu = send(gb, 0, 0, up)
-    bd = send(gb, 0, 0, down)
     mu.wait_recv()
     mu2 = send(gm, 3, 0, up)
     share(("gm", 3, 0, ""), gm, 3, 0)
     md.wait_recv()
     share(("gm", 1, 0, ""), gm, 1, 0)
-    share(("gb", 0, 0, ""), gb, 0, 0)
-
-    @pl.loop(0, TA // 128)
-    def _(t):
-        at = pl.ds(pl.multiple_of(t * 128, 128), 128)
-        mine_a[:, at] = slope(pre[:, at]).astype(BF16)
-
-    fa = send(ga, 0, 0, flip)
+    z4_a = to_row(0, z3_a)
+    z3_b = over_col(1, z2_b)
+    fb = send(gb, 0, 0, flip)
+    fa.wait_recv()
+    fau = send(ga, 0, 1, up)
+    fad = send(ga, 0, 1, down)
+    share(("ga", 0, 1, ""), ga, 0, 1)
     mfd.wait_recv()
     mfd2 = send(gm, 1, 1, down)
     share(("gm", 1, 1, ""), gm, 1, 1)
     mfu.wait_recv()
     share(("gm", 3, 1, ""), gm, 3, 1)
-    share(("ga", 0, 0, ""), ga, 0, 0)
-    mine = pl.ds(pl.multiple_of(here * 16, 16), 16)
-    part = z2[mine, :].astype(F32)
-    for index, copy in enumerate(z2_copies):
-        copy.wait_recv()
-        part = part + z2_recv[index].astype(F32)
-    z3[col] = part.astype(BF16)
-    z3_copies = [remote(z3.at[col], z3.at[col], at_col(*peer)) for peer in col_peers]
-    au = send(ga, 0, 0, up)
-    ad = send(ga, 0, 0, down)
-    fb = send(gb, 0, 0, flip)
     bu.wait_recv()
-    bu2 = send(gb, 3, 0, up, top)
+    f_m = send(gb, 3, 0, flip)
     share(("gb", 3, 0, ""), gb, 3, 0)
     bd.wait_recv()
+    f_p = send(gb, 1, 0, flip)
+    share(("gb", 1, 0, ""), gb, 1, 0)
+    z4_b = to_row(1, z3_b)
+    bu2 = send(gb, 3, 0, up, top)
     bd2 = send(gb, 1, 0, down, low)
-    share(("gb", 1, 0, ""), gb, 1, 0)
-    for copy in z3_copies:
-        copy.wait_recv()
-    total = z3[0].astype(F32)
-    for index in range(1, 8):
-        total = total + z3[index].astype(F32)
-    field[mine, :] = total.astype(BF16)
-    z4_copies = [
-        remote(field.at[mine], field.at[mine], at_row(dz, dh, 0)) for dz, dh in chip_peers
-    ]
-    f_m = send(gb, 3, 0, flip)
-    f_p = send(gb, 1, 0, flip)
-    fa.wait_recv()
-    fau = send(ga, 0, 1, up)
-    fad = send(ga, 0, 1, down)
-    share(("ga", 0, 1, ""), ga, 0, 1)
     au.wait_recv()
     au2 = send(ga, 3, 0, up)
     share(("ga", 3, 0, ""), ga, 3, 0)
@@ -436,17 +451,9 @@
     share(("ga", 1, 0, ""), ga, 1, 0)
     fb.wait_recv()
     share(("gb", 0, 1, ""), gb, 0, 1)
-    bu2.wait_recv()
-    f_top = send(gb, 2, 0, flip, top)
-    share(("gb", 2, 0, "top"), gb, 2, 0, top)
-    bd2.wait_recv()
-    f_low = send(gb, 2, 0, flip, low)
-    share(("gb", 2, 0, "low"), gb, 2, 0, low)
     mu2.wait_recv()
     share(("gm", 2, 0, ""), gm, 2, 0)
-    mfd2.wait_recv()
-    share(("gm", 2, 1, ""), gm, 2, 1)
-    for copy in z4_copies:
+    for copy in z4_a + z4_b:
         copy.wait_recv()
 
     token = lax.broadcasted_iota(jnp.int32, (1, TOK), 1)
@@ -477,6 +484,14 @@
         rows_buf[index : index + 1, :] = pred[:, index * STRIP : (index + 1) * STRIP]
     pred_all[c] = rows_buf[...]
     pred_copy = remote(pred_all.at[c], pred_all.at[c], partner)
+    mfd2.wait_recv()
+    share(("gm", 2, 1, ""), gm, 2, 1)
+    bu2.wait_recv()
+    f_top = send(gb, 2, 0, flip, top)
+    share(("gb", 2, 0, "top"), gb, 2, 0, top)
+    bd2.wait_recv()
+    f_low = send(gb, 2, 0, flip, low)
+    share(("gb", 2, 0, "low"), gb, 2, 0, low)
     fad.wait_recv()
     fad2 = send(ga, 1, 1, down)
     share(("ga", 1, 1, ""), ga, 1, 1)

time: 109 us -> 111 us (1.018)
  Pallas kernels: 106 us -> 109 us
    pallas_call x1, Pallas kernels: 100 us -> 103 us  [on_device(): pl.pallas_call(step_kernel, name='mlp_step', out_shape=[jax.ShapeDtypeStr...]
where the time goes in v8:
time: 111 us
  Pallas kernels  109 us (98%)
  between operations  2.4 us (2%)
    pallas_call x1, Pallas kernels, on_device(): pl.pallas_call(step_kernel, name='mlp_step', out_shape=[jax.ShapeDtypeStr...  103 us
    pallas_call x1, Pallas kernels, on_device(): pl.pallas_call(weight_kernel, name='weight_grads', out_shape=[jax.ShapeDt...  5.59 us

profile of v8, /device:TPU:1, one launch (start us, length us, event | category | flops | bytes accessed | tf_op | source)
XLA Modules:
  0.0 111.1 jit_solution(7503653786415691086)
XLA Ops:
  0.6 103.1 %mlp_step.1 = (f32[384,3072]{1,0:T(8,128)}, bf16[3072,256]{1,0:T(8,128)(2,1)}, f32[1,1]{1,0:T(1,128)}) custom-call(bf16[128,384]{1,0:T(8,128)(2,1)} %tok_hbm.1, f32[384]{0:T(512)} %gain_ref.1, bf16[384,3072]{1,0:T(8,128)(2,1)} %wup_hbm.1, bf16[3072,384]{1,0:T(8,128)(2,1)} %wdn_hbm.1, bf16[384,256]{1,0:T(8,128)(2,1)} %proj_hbm.3, ...), custom_call_target="tpu_custom_call" | custom-call | flops 6000000000 | bytes 16777216 | tf_op jit(solution)/shard_map/mlp_step/pallas_call | solution.py:657
  103.7 5.6 %weight_grads.1 = (f32[384,3072]{1,0:T(8,128)}, f32[3072,384]{1,0:T(8,128)}) custom-call(bf16[3072,256]{1,0:T(8,128)(2,1)} %get-tuple-element.8.gh_hbm, bf16[384,256]{1,0:T(8,128)(2,1)} %proj_hbm.3, f32[384,3072]{1,0:T(8,128)} %get-tuple-element.9.up_hbm), custom_call_target="tpu_custom_call" | custom-call | flops 600000000 | bytes 16777216 | tf_op jit(solution)/shard_map/weight_grads/pallas_call | solution.py:731

commit v9 on v7

--- a/solution.py
+++ b/solution.py
@@ -315,7 +315,8 @@
     mu = send(gm, 0, 0, up)
     md = send(gm, 0, 0, down)
     share(("gm", 0, 0, ""), gm, 0, 0)
-    x_proj = tn(proj_ref[...], xall[col])
+    zc[...] = jnp.zeros_like(zc)
+    zc[:, pl.ds(pl.multiple_of(col * STRIP, STRIP), STRIP)] = tn(proj_ref[...], xall[col])
 
     conv_copy.wait()
     head = head_ref[...]
@@ -329,35 +330,39 @@
         jnp.sum(jnp.where(lane == sub + first_channel, head, 0.0), axis=1, keepdims=True), (128, 128)
     )
 
-    b_copies[0].wait_recv()
+    mine_a, mine_b = ga.at[slot(0, 0)], gb.at[slot(0, 0)]
+
+    def hidden(part):
+        @pl.loop(0, TA // 256)
+        def _(t):
+            at = pl.ds(pl.multiple_of(part * TA + t * 256, 256), 256)
+            value = pre[:, at]
+            value = (value * cdf(value)).astype(BF16)
+            hid[:, at] = value
+            zc[:, at] = zc[:, at] + tn(m_own[...], value)
+
     a_flip.wait_recv()
     pre[:, :TA] = (
         p_a[z, h].astype(F32) + a2[0, h].astype(F32) + a2[1, h].astype(F32) + a3[...].astype(F32)
     )
+    hidden(0)
+
+    @pl.loop(0, TA // 128)
+    def _(t):
+        at = pl.ds(pl.multiple_of(t * 128, 128), 128)
+        mine_a[:, at] = slope(pre[:, at]).astype(BF16)
+
+    b_copies[0].wait_recv()
     b_up2.wait_recv()
     b_down2.wait_recv()
     pre[:, TA:] = (
         p_b[z, h].astype(F32) + b1[z].astype(F32) + b3[0].astype(F32) + b3[1].astype(F32)
     )
-
-    @pl.loop(0, TOK // 128)
-    def _(t):
-        at = pl.ds(pl.multiple_of(t * 128, 128), 128)
-        value = pre[:, at]
-        hid[:, at] = (value * cdf(value)).astype(BF16)
-
-    @pl.loop(0, TOK // 256)
-    def _(t):
-        at = pl.ds(pl.multiple_of(t * 256, 256), 256)
-        zc[:, at] = tn(m_own[...], hid[:, at])
-
-    strip = pl.ds(pl.multiple_of(col * STRIP, STRIP), STRIP)
-    zc[:, strip] = zc[:, strip] + x_proj
+    hidden(1)
 
     z1[...] = zc[pl.ds(pl.multiple_of(other * 128, 128), 128), :].astype(BF16)
     z1_copy = remote(z1, z1_recv, partner)
 
-    mine_a, mine_b = ga.at[slot(0, 0)], gb.at[slot(0, 0)]
     mf.wait_recv()
     mfu = send(gm, 0, 1, up)
     mfd = send(gm, 0, 1, down)
@@ -385,11 +390,6 @@
     md.wait_recv()
     share(("gm", 1, 0, ""), gm, 1, 0)
     share(("gb", 0, 0, ""), gb, 0, 0)
-
-    @pl.loop(0, TA // 128)
-    def _(t):
-        at = pl.ds(pl.multiple_of(t * 128, 128), 128)
-        mine_a[:, at] = slope(pre[:, at]).astype(BF16)
 
     fa = send(ga, 0, 0, flip)
     mfd.wait_recv()

time: 109 us -> 108 us (level)
  no operation moved by 1% of the time
where the time goes in v9:
time: 108 us
  Pallas kernels  106 us (98%)
  between operations  2.4 us (2%)
    pallas_call x1, Pallas kernels, on_device(): pl.pallas_call(step_kernel, name='mlp_step', out_shape=[jax.ShapeDtypeStr...  100 us
    pallas_call x1, Pallas kernels, on_device(): pl.pallas_call(weight_kernel, name='weight_grads', out_shape=[jax.ShapeDt...  5.59 us

profile of v9, /device:TPU:1, one launch (start us, length us, event | category | flops | bytes accessed | tf_op | source)
XLA Modules:
  0.0 108.4 jit_solution(272002600077268529)
XLA Ops:
  0.6 100.4 %mlp_step.1 = (f32[384,3072]{1,0:T(8,128)}, bf16[3072,256]{1,0:T(8,128)(2,1)}, f32[1,1]{1,0:T(1,128)}) custom-call(bf16[128,384]{1,0:T(8,128)(2,1)} %tok_hbm.1, f32[384]{0:T(512)} %gain_ref.1, bf16[384,3072]{1,0:T(8,128)(2,1)} %wup_hbm.1, bf16[3072,384]{1,0:T(8,128)(2,1)} %wdn_hbm.1, bf16[384,256]{1,0:T(8,128)(2,1)} %proj_hbm.3, ...), custom_call_target="tpu_custom_call" | custom-call | flops 6000000000 | bytes 16777216 | tf_op jit(solution)/shard_map/mlp_step/pallas_call | solution.py:642
  101.0 5.6 %weight_grads.1 = (f32[384,3072]{1,0:T(8,128)}, f32[3072,384]{1,0:T(8,128)}) custom-call(bf16[3072,256]{1,0:T(8,128)(2,1)} %get-tuple-element.8.gh_hbm, bf16[384,256]{1,0:T(8,128)(2,1)} %proj_hbm.3, f32[384,3072]{1,0:T(8,128)} %get-tuple-element.9.up_hbm), custom_call_target="tpu_custom_call" | custom-call | flops 600000000 | bytes 16777216 | tf_op jit(solution)/shard_map/weight_grads/pallas_call | solution.py:716

commit v10 on v7

--- a/solution.py
+++ b/solution.py
@@ -525,9 +525,10 @@
         hid[...], gz[pl.ds(second_channel, 128), :]
     ).astype(BF16)
     local(gh_own, gh_out.at[own_rows(0, 0)])
-    gh_copies = [
-        remote(gh_own, gh_out.at[own_rows(0, 0)], at_row(dz, dh, 0)) for dz, dh in chip_peers
-    ]
+    gh_flip = {0: remote(gh_own, gh_out.at[own_rows(0, 0)], flip)}
+    gh_copies = {
+        dz: remote(gh_own, gh_out.at[own_rows(0, 0)], at_row(dz, 0, 0)) for dz in (2, 1, 3)
+    }
     gh_pair = [remote(gh_own, gh_out.at[own_rows(0, 0)], partner)]
     def ready(dz):
         for key, copy in pair.items():
@@ -573,12 +574,17 @@
     column(1)
     fad2.wait_recv()
     share(("ga", 2, 1, ""), ga, 2, 1)
+    for dz, copy in gh_copies.items():
+        copy.wait_recv()
+        came = gh_out.at[own_rows(-dz, 0)]
+        gh_flip[dz] = remote(came, came, flip)
+        gh_pair.append(remote(came, came, partner))
     ready(2)
     column(2)
 
-    for (dz, dh), copy in zip(chip_peers, gh_copies):
-        copy.wait_recv()
-        came = gh_out.at[own_rows(-dz, dh)]
+    for dz, copy in gh_flip.items():
+        copy.wait_recv()
+        came = gh_out.at[own_rows(-dz, 1)]
         gh_pair.append(remote(came, came, partner))
     for copy in gh_pair:
         copy.wait_recv()

time: 109 us -> 112 us (1.028)
  Pallas kernels: 106 us -> 109 us
    pallas_call x1, Pallas kernels: 100 us -> 104 us  [on_device(): pl.pallas_call(step_kernel, name='mlp_step', out_shape=[jax.ShapeDtypeStr...]
where the time goes in v10:
time: 112 us
  Pallas kernels  109 us (97%)
  between operations  2.4 us (2%)
    pallas_call x1, Pallas kernels, on_device(): pl.pallas_call(step_kernel, name='mlp_step', out_shape=[jax.ShapeDtypeStr...  104 us
    pallas_call x1, Pallas kernels, on_device(): pl.pallas_call(weight_kernel, name='weight_grads', out_shape=[jax.ShapeDt...  5.59 us

profile of v10, /device:TPU:1, one launch (start us, length us, event | category | flops | bytes accessed | tf_op | source)
XLA Modules:
  0.0 111.7 jit_solution(1096388987427043686)
XLA Ops:
  0.6 103.7 %mlp_step.1 = (f32[384,3072]{1,0:T(8,128)}, bf16[3072,256]{1,0:T(8,128)(2,1)}, f32[1,1]{1,0:T(1,128)}) custom-call(bf16[128,384]{1,0:T(8,128)(2,1)} %tok_hbm.1, f32[384]{0:T(512)} %gain_ref.1, bf16[384,3072]{1,0:T(8,128)(2,1)} %wup_hbm.1, bf16[3072,384]{1,0:T(8,128)(2,1)} %wdn_hbm.1, bf16[384,256]{1,0:T(8,128)(2,1)} %proj_hbm.3, ...), custom_call_target="tpu_custom_call" | custom-call | flops 6000000000 | bytes 16777216 | tf_op jit(solution)/shard_map/mlp_step/pallas_call | solution.py:648
  104.3 5.6 %weight_grads.1 = (f32[384,3072]{1,0:T(8,128)}, f32[3072,384]{1,0:T(8,128)}) custom-call(bf16[3072,256]{1,0:T(8,128)(2,1)} %get-tuple-element.8.gh_hbm, bf16[384,256]{1,0:T(8,128)(2,1)} %proj_hbm.3, f32[384,3072]{1,0:T(8,128)} %get-tuple-element.9.up_hbm), custom_call_target="tpu_custom_call" | custom-call | flops 600000000 | bytes 16777216 | tf_op jit(solution)/shard_map/weight_grads/pallas_call | solution.py:722

commit v11 on v7

--- a/solution.py
+++ b/solution.py
@@ -477,11 +477,6 @@
         rows_buf[index : index + 1, :] = pred[:, index * STRIP : (index + 1) * STRIP]
     pred_all[c] = rows_buf[...]
     pred_copy = remote(pred_all.at[c], pred_all.at[c], partner)
-    fad.wait_recv()
-    fad2 = send(ga, 1, 1, down)
-    share(("ga", 1, 1, ""), ga, 1, 1)
-    fau.wait_recv()
-    share(("ga", 3, 1, ""), ga, 3, 1)
 
     @pl.loop(0, TOK // 128)
     def _(t):
@@ -517,6 +512,11 @@
 
     half_z = gz.at[pl.ds(first_channel, 128)]
     gz_copy = remote(half_z, half_z, partner)
+    fad.wait_recv()
+    fad2 = send(ga, 1, 1, down)
+    share(("ga", 1, 1, ""), ga, 1, 1)
+    fau.wait_recv()
+    share(("ga", 3, 1, ""), ga, 3, 1)
 
     second_channel = pl.multiple_of(other * 128, 128)
     gh_own[:, pl.ds(first_channel, 128)] = nt(hid[...], half_z[...]).astype(BF16)

time: 109 us -> 109 us (level)
  no operation moved by 1% of the time
where the time goes in v11:
time: 109 us; the launch traced here: 108 us
  Pallas kernels  106 us (97%)
  between operations  2.4 us (2%)
    pallas_call x1, Pallas kernels, on_device(): pl.pallas_call(step_kernel, name='mlp_step', out_shape=[jax.ShapeDtypeStr...  100 us
    pallas_call x1, Pallas kernels, on_device(): pl.pallas_call(weight_kernel, name='weight_grads', out_shape=[jax.ShapeDt...  5.59 us

profile of v11, /device:TPU:1, one launch (start us, length us, event | category | flops | bytes accessed | tf_op | source)
XLA Modules:
  0.0 108.4 jit_solution(14728753484258504620)
XLA Ops:
  0.6 100.4 %mlp_step.1 = (f32[384,3072]{1,0:T(8,128)}, bf16[3072,256]{1,0:T(8,128)(2,1)}, f32[1,1]{1,0:T(1,128)}) custom-call(bf16[128,384]{1,0:T(8,128)(2,1)} %tok_hbm.1, f32[384]{0:T(512)} %gain_ref.1, bf16[384,3072]{1,0:T(8,128)(2,1)} %wup_hbm.1, bf16[3072,384]{1,0:T(8,128)(2,1)} %wdn_hbm.1, bf16[384,256]{1,0:T(8,128)(2,1)} %proj_hbm.3, ...), custom_call_target="tpu_custom_call" | custom-call | flops 6000000000 | bytes 16777216 | tf_op jit(solution)/shard_map/mlp_step/pallas_call | solution.py:642
  101.1 5.6 %weight_grads.1 = (f32[384,3072]{1,0:T(8,128)}, f32[3072,384]{1,0:T(8,128)}) custom-call(bf16[3072,256]{1,0:T(8,128)(2,1)} %get-tuple-element.8.gh_hbm, bf16[384,256]{1,0:T(8,128)(2,1)} %proj_hbm.3, f32[384,3072]{1,0:T(8,128)} %get-tuple-element.9.up_hbm), custom_call_target="tpu_custom_call" | custom-call | flops 600000000 | bytes 16777216 | tf_op jit(solution)/shard_map/weight_grads/pallas_call | solution.py:716

commit v12 on v9

--- a/solution.py
+++ b/solution.py
@@ -352,6 +352,8 @@
         at = pl.ds(pl.multiple_of(t * 128, 128), 128)
         mine_a[:, at] = slope(pre[:, at]).astype(BF16)
 
+    fa = send(ga, 0, 0, flip)
+
     b_copies[0].wait_recv()
     b_up2.wait_recv()
     b_down2.wait_recv()
@@ -391,7 +393,6 @@
     share(("gm", 1, 0, ""), gm, 1, 0)
     share(("gb", 0, 0, ""), gb, 0, 0)
 
-    fa = send(ga, 0, 0, flip)
     mfd.wait_recv()
     mfd2 = send(gm, 1, 1, down)
     share(("gm", 1, 1, ""), gm, 1, 1)

time: 108 us -> 108 us (level)
  no operation moved by 1% of the time
where the time goes in v12:
time: 108 us
  Pallas kernels  106 us (98%)
  between operations  2.4 us (2%)
    pallas_call x1, Pallas kernels, on_device(): pl.pallas_call(step_kernel, name='mlp_step', out_shape=[jax.ShapeDtypeStr...  100 us
    pallas_call x1, Pallas kernels, on_device(): pl.pallas_call(weight_kernel, name='weight_grads', out_shape=[jax.ShapeDt...  5.59 us

profile of v12, /device:TPU:1, one launch (start us, length us, event | category | flops | bytes accessed | tf_op | source)
XLA Modules:
  0.0 108.2 jit_solution(18190970724498576125)
XLA Ops:
  0.6 100.2 %mlp_step.1 = (f32[384,3072]{1,0:T(8,128)}, bf16[3072,256]{1,0:T(8,128)(2,1)}, f32[1,1]{1,0:T(1,128)}) custom-call(bf16[128,384]{1,0:T(8,128)(2,1)} %tok_hbm.1, f32[384]{0:T(512)} %gain_ref.1, bf16[384,3072]{1,0:T(8,128)(2,1)} %wup_hbm.1, bf16[3072,384]{1,0:T(8,128)(2,1)} %wdn_hbm.1, bf16[384,256]{1,0:T(8,128)(2,1)} %proj_hbm.3, ...), custom_call_target="tpu_custom_call" | custom-call | flops 6000000000 | bytes 16777216 | tf_op jit(solution)/shard_map/mlp_step/pallas_call | solution.py:643
  100.8 5.6 %weight_grads.1 = (f32[384,3072]{1,0:T(8,128)}, f32[3072,384]{1,0:T(8,128)}) custom-call(bf16[3072,256]{1,0:T(8,128)(2,1)} %get-tuple-element.8.gh_hbm, bf16[384,256]{1,0:T(8,128)(2,1)} %proj_hbm.3, f32[384,3072]{1,0:T(8,128)} %get-tuple-element.9.up_hbm), custom_call_target="tpu_custom_call" | custom-call | flops 600000000 | bytes 16777216 | tf_op jit(solution)/shard_map/weight_grads/pallas_call | solution.py:717
